TPU v7x, 256 devices: a whole 4x4x8 slice. The times are simulated.
256 devices in a mesh: dp: 16 (over y, x_lo, core), head: 16 (over x_hi, z).
Axes of the slice: x: 4 (x_hi: 2, x_lo: 2; x = x_hi * 2 + x_lo), y: 4, z: 8, core: 2. Of those that a mesh axis runs over, the one named last changes fastest.
Arguments:
- query_rows: bfloat16 [16384, 8192], P('dp', 'head'), may hold values from -126 to 126
- key_rows: bfloat16 [16384, 1024], P('dp'), may hold values from -6 to 6
- value_rows: bfloat16 [16384, 1024], P('dp'), may hold values from -6 to 6
- out_weight: bfloat16 [8192, 8192], P('head'), may hold values from -0.0625 to 0.0625
- prompt_lengths: int32 [16, 4], P('dp'), may hold values from 1 to 512, 1024 in all within a row
- cache_pool: bfloat16 [2048, 2, 16, 1024], P('dp', None, None, 'head'), may hold values from -6 to 6
- victim_blocks: int32 [1024], P('dp'), may hold values from 0 to 127
- destinations: int32 [1024, 1], P('dp'), may hold values from 0 to 15; in each aligned block of 64 rows (0 to 63, 64 to 127, ...) at most 8 rows name the same one
- free_slots: int32 [16, 128], P('dp'), may hold values from 0 to 127, each once within a row
Outputs:
- attended: bfloat16 [16384, 8192], P(('dp', 'head'))
- new_pool: bfloat16 [2048, 2, 16, 1024], P('dp', None, None, 'head')
Inputs may be any that keep to these rules, and one draw needn't show every extreme that they name: `destinations`: in the 64 victim blocks of one replica no destination is named more than 8 times. `victim_blocks`: pool blocks of the sending replica. `free_slots`: each row is an order of the 128 slots. `prompt_lengths`: each row sums to 1024.
All inputs are finite; a program needn't handle non-finite values.
Results may differ from a plain program's by a relative error of at most 0.019.
Values may be sent and summed in bfloat16 or wider, within the bound.
No kernel may reach another device: no remote copies, remote signals or barrier semaphores. Data moves between devices by JAX's collectives and lax.ppermute only.
A program may use at most 128 MiB of HBM per device.

v0:
```python
import functools
import math

import jax
import jax.numpy as jnp
from jax import lax
from jax.experimental import pallas as pl
from jax.experimental.pallas import tpu as pltpu
from jax.sharding import PartitionSpec as P

HD = 128
KVH = 8
BT = 16
NZ = 8
NY = 4
QB = 256
SPAN = 768
FIRST = 2048
GROUPS = ((2048, 5120), (5120, 8192))
Z_GROUPS = [[a * 8 + z for z in range(8)] for a in range(2)]
TILE = 1024
VMEM = 56 * 1024 * 1024
BF = jnp.bfloat16
F32 = jnp.float32
X_SWAP = [(i, (i + 8) % 16) for i in range(16)]
CORE_SWAP = [(i, i ^ 1) for i in range(16)]
LO_SWAP = [(i, i ^ 2) for i in range(16)]

def y_shift(k):
    return [(y * 4 + r, (y + k) % NY * 4 + r) for y in range(NY) for r in range(4)]


def attend_kernel(side, info, lengths, q_ref, k_ref, v_ref, o_ref):
    block = info[side] * 2 + pl.program_id(0)

    def attend(span):
        base = jnp.maximum(block - 2, 0) * QB
        rows = block * QB + lax.broadcasted_iota(jnp.int32, (QB, 1), 0)
        start = jnp.zeros((QB, 1), jnp.int32)
        end = 0
        for s in range(lengths.shape[1]):
            end = end + lengths[0, s]
            start = jnp.where(rows >= end, end, start)
        cols = base + lax.broadcasted_iota(jnp.int32, (QB, span), 1)
        bias = jnp.where((cols >= start) & (cols <= rows), 0.0, -1e30)
        keys = k_ref[pl.ds(pl.multiple_of(base, QB), span), :]
        values = jnp.concatenate(
            [v_ref[pl.ds(pl.multiple_of(base, QB), span), :], jnp.ones((span, HD), BF)], axis=1
        )
        for h in range(q_ref.shape[1] // HD):
            q = q_ref[:, h * HD : (h + 1) * HD]
            s = lax.dot_general(q, keys, (((1,), (1,)), ((), ())), preferred_element_type=F32) + bias
            top = jnp.max(s, axis=1, keepdims=True)
            e = jnp.exp2((s - top) * (math.log2(math.e) / math.sqrt(HD)))
            o = jnp.dot(e.astype(BF), values, preferred_element_type=F32)
            o_ref[:, h * HD : (h + 1) * HD] = (o[:, :HD] / o[:, HD:]).astype(BF)

    pl.when(block == 0)(lambda: attend(QB))
    pl.when(block == 1)(lambda: attend(2 * QB))
    pl.when(block >= 2)(lambda: attend(SPAN))


def attend_half(side, info, prompt_lengths, query_rows, key_rows, value_rows):
    count, width = query_rows.shape
    return pl.pallas_call(
        functools.partial(attend_kernel, side),
        grid_spec=pltpu.PrefetchScalarGridSpec(
            num_scalar_prefetch=2,
            grid=(2,),
            in_specs=[
                pl.BlockSpec((QB, width), lambda i, info, _: (info[side] * 2 + i, 0)),
                pl.BlockSpec((count, HD), lambda i, info, _: (0, info[2])),
                pl.BlockSpec((count, HD), lambda i, info, _: (0, info[2])),
            ],
            out_specs=pl.BlockSpec((QB, width), lambda i, info, _: (i, 0)),
        ),
        out_shape=jax.ShapeDtypeStruct((2 * QB, width), BF),
        compiler_params=pltpu.CompilerParams(vmem_limit_bytes=VMEM),
        cost_estimate=pl.CostEstimate(
            flops=4 * 2 * QB * SPAN * width, bytes_accessed=2 << 20, transcendentals=8 * QB * SPAN
        ),
    )(info, prompt_lengths, query_rows, key_rows, value_rows)


def after(value, *earlier):
    return lax.optimization_barrier((value, *earlier))[0]


def project_kernel(kept_ref, given_ref, w_ref, own_ref, other_ref, *refs):
    o_ref = refs[-1]
    half = own_ref.shape[0]
    acc = jnp.dot(kept_ref[...], w_ref[...], preferred_element_type=F32)
    acc += jnp.dot(given_ref[:, :half], own_ref[...], preferred_element_type=F32)
    acc += jnp.dot(given_ref[:, half:], other_ref[...], preferred_element_type=F32)
    o_ref[...] = acc.astype(BF)


def project(kept, given, out_weight, group, own, other, filled):
    rows, depth = kept.shape
    first, last = GROUPS[group]
    base = GROUPS[0][0]
    return pl.pallas_call(
        project_kernel,
        grid=((last - first) // TILE,),
        in_specs=[
            pl.BlockSpec((rows, depth), lambda i: (0, 0)),
            pl.BlockSpec((rows, depth), lambda i: (0, 0)),
            pl.BlockSpec((depth, TILE), lambda i: (0, first // TILE + i)),
            pl.BlockSpec((depth // 2, TILE), lambda i: (0, i)),
            pl.BlockSpec((depth // 2, TILE), lambda i: (0, i)),
        ]
        + [pl.BlockSpec(memory_space=pl.ANY)] * len(filled),
        out_specs=pl.BlockSpec((rows, TILE), lambda i: (0, (first - base) // TILE + i)),
        out_shape=jax.ShapeDtypeStruct((rows, GROUPS[-1][1] - base), BF),
        input_output_aliases={5: 0} if filled else {},
        compiler_params=pltpu.CompilerParams(vmem_limit_bytes=VMEM),
        cost_estimate=pl.CostEstimate(
            flops=4 * rows * depth * (last - first), bytes_accessed=6 * depth * (last - first), transcendentals=0
        ),
    )(kept, given, out_weight, own, other, *filled)


def project_first_kernel(kept_ref, theirs_ref, w_ref, o_ref):
    own = pl.program_id(0) == 0
    rows = jnp.where(own, kept_ref[...], theirs_ref[...])
    o_ref[...] = jnp.dot(rows, w_ref[...], preferred_element_type=F32).astype(BF)


def project_first(kept, theirs, out_weight, size):
    rows, depth = kept.shape
    tiles = size // TILE
    return pl.pallas_call(
        project_first_kernel,
        grid=(2, tiles),
        in_specs=[
            pl.BlockSpec((rows, depth), lambda h, i: (0, 0)),
            pl.BlockSpec((rows, depth), lambda h, i: (0, 0)),
            pl.BlockSpec((depth, TILE), lambda h, i: (0, i)),
        ],
        out_specs=pl.BlockSpec((rows, TILE), lambda h, i: (0, h * tiles + i)),
        out_shape=jax.ShapeDtypeStruct((rows, 2 * size), BF),
        compiler_params=pltpu.CompilerParams(vmem_limit_bytes=VMEM),
        cost_estimate=pl.CostEstimate(
            flops=4 * rows * depth * size, bytes_accessed=3 * depth * size * 2, transcendentals=0
        ),
    )(kept, theirs, out_weight)


def sum_over_z(part):
    return lax.psum_scatter(part, "head", scatter_dimension=0, axis_index_groups=Z_GROUPS, tiled=True)


def migrate(key_rows, value_rows, cache_pool, victim_blocks, targets, free_order):
    count, width = key_rows.shape[0], cache_pool.shape[3]
    pool, written = cache_pool.shape[0], count // BT
    at = lax.axis_index("head") * width
    me = lax.axis_index("dp")
    y, low = me // 4, me % 4
    rows = [after(lax.dynamic_slice_in_dim(a, at, width, 1), targets) for a in (key_rows, value_rows)]
    span = jnp.stack([a.reshape(written, BT, width) for a in rows], axis=1)
    r = jnp.arange(16, dtype=jnp.int32)
    target_place = ((targets // 4 - y) % NY) * 4 + ((targets % 4) ^ low)
    same = targets[:, None] == targets[None, :]
    victims = victim_blocks.shape[0]
    order = jnp.arange(victims, dtype=jnp.int32)
    local_rank = jnp.sum((same & (order[None, :] < order[:, None])).astype(jnp.int32), axis=1)
    slot_of = target_place * 8 + local_rank
    lanes = jnp.arange(128, dtype=jnp.int32)
    picks = (slot_of[None, :] == lanes[:, None]).astype(BF)
    blocks = (victim_blocks[:, None] == jnp.arange(pool, dtype=jnp.int32)[None, :]).astype(BF)
    pick = jnp.dot(picks, blocks, preferred_element_type=F32).astype(BF)
    empty = 1.0 - jnp.sum(pick.astype(F32), axis=1)
    sending = jnp.einsum("sb,bktf->sktf", pick[:, :written], span, preferred_element_type=F32)
    sending = sending + jnp.einsum("sb,bktf->sktf", pick[:, written:], cache_pool[written:], preferred_element_type=F32)
    sending = (sending + 256.0 * empty[:, None, None, None]).astype(BF)
    b = sending.reshape(NY, 2, 2, 8 * 2 * BT * width)
    b = jnp.stack([b[:, :, 0], lax.ppermute(b[:, :, 1], "dp", CORE_SWAP)], axis=2)
    b = jnp.stack([b[:, 0], lax.ppermute(b[:, 1], "dp", LO_SWAP)], axis=1)
    b = jnp.stack([b[0]] + [lax.ppermute(b[k], "dp", y_shift(k)) for k in (1, 2, 3)])
    arrived = b.reshape(128, 2, BT, width)
    valid = (arrived[:, 0, 0, 0].astype(F32) < 100.0).reshape(16, 8)
    source = ((y - r // 4) % NY) * 4 + ((r % 4) ^ low)
    counts = jnp.sum(valid.astype(jnp.int32), axis=1)
    before = jnp.sum(jnp.where(source[None, :] < source[:, None], counts[None, :], 0), axis=1)
    ranks = before[:, None] + jnp.arange(8, dtype=jnp.int32)[None, :]
    rank_of_slot = jnp.sum(
        (free_order[None, :] == jnp.arange(pool, dtype=jnp.int32)[:, None]) * jnp.arange(pool, dtype=jnp.int32)[None, :],
        axis=1,
    )
    hits = (ranks.reshape(128, 1) == rank_of_slot[None, :]) & valid.reshape(128, 1)
    taken = jnp.sum(hits.astype(jnp.int32), axis=0) > 0
    fresh = jnp.einsum(
        "sktf,sb->bktf", jnp.where(valid.reshape(128, 1, 1, 1), arrived, 0), hits.astype(BF), preferred_element_type=F32
    ).astype(BF)
    sectioned = lax.dynamic_update_slice_in_dim(cache_pool, span, 0, 0)
    return jnp.where(taken[:, None, None, None], fresh, sectioned)


def on_device(
    query_rows,
    key_rows,
    value_rows,
    out_weight,
    prompt_lengths,
    cache_pool,
    victim_blocks,
    destinations,
    free_slots,
):
    head, me = lax.axis_index("head"), lax.axis_index("dp")
    z, hi = head % NZ, head // NZ
    y, core = me // 4, me % 2
    depth = out_weight.shape[0]
    eighth = depth // 8
    slab = lax.dynamic_slice_in_dim(out_weight, (y * 2 + core) * eighth, eighth, 0)
    kv = head * KVH // lax.axis_size("head")
    place = jnp.arange(depth, dtype=jnp.int32)
    slot = place // eighth
    taken_from = (((y + slot % NY) % NY) * 2 + (core ^ (slot // NY))) * eighth + place % eighth
    order = (place[:, None] == taken_from[None, :]).astype(BF)
    info = jnp.stack([1 - hi, hi, kv])
    count = query_rows.shape[0] // 2
    got = [lax.ppermute(slab[:, slice(*GROUPS[0])], "head", X_SWAP)]
    opposite = lax.dynamic_slice_in_dim(after(out_weight, got[0]), ((y + 2) % NY * 2 + core) * eighth, eighth, 0)
    theirs = attend_half(0, info, prompt_lengths, query_rows, key_rows, value_rows)
    came = lax.ppermute(theirs, "head", X_SWAP)
    kept = attend_half(1, info, after(prompt_lengths, theirs, got[0]), query_rows, key_rows, value_rows)
    given = jnp.dot(came, order, preferred_element_type=F32).astype(BF)
    part = project_first(kept, theirs, out_weight, FIRST)
    firsts = sum_over_z(part).reshape(count // NZ, 2 * FIRST)
    both = jnp.concatenate([slab[:, slice(*GROUPS[1])], opposite[:, slice(*GROUPS[1])]], axis=0)
    got.append(lax.ppermute(after(both, got[0]), "head", X_SWAP))
    sides, before = [], ()
    for i in range(len(GROUPS)):
        piece, across = got[i][:eighth], got[i][eighth:]
        piece = after(piece, theirs, *before)
        near, far = (lax.ppermute(piece, "dp", y_shift(k)) for k in (1, -1))
        if i == 0:
            across = lax.ppermute(piece, "dp", y_shift(2))
        before = (near, far, across)
        own = after(jnp.concatenate([piece, far, across, near], axis=0), came)
        sides.append((own, lax.ppermute(own, "dp", CORE_SWAP)))
    part = project(kept, after(given, got[1], *before), out_weight, 0, *sides[0], ())
    part = project(kept, given, out_weight, 1, *sides[1], (part,))
    rest = sum_over_z(part)
    swapped = lax.ppermute(firsts[:, FIRST:], "head", X_SWAP)
    begin = (firsts[:, :FIRST].astype(F32) + swapped.astype(F32)).astype(BF)
    attended = jnp.zeros((count // NZ, out_weight.shape[1]), BF)
    for lo, piece in ((0, begin), (FIRST, rest)):
        attended = lax.dynamic_update_slice(attended, piece, (0, lo))
    victim_blocks, targets, free_order, _ = lax.optimization_barrier(
        (victim_blocks, destinations[:, 0], free_slots[0], part)
    )
    new_pool = migrate(key_rows, value_rows, cache_pool, victim_blocks, targets, free_order)
    return (attended, new_pool)


def solution(mesh):
    return jax.shard_map(
        on_device,
        mesh=mesh,
        in_specs=(
            P("dp", "head"),
            P("dp", None),
            P("dp", None),
            P("head", None),
            P("dp", None),
            P("dp", None, None, "head"),
            P("dp"),
            P("dp", None),
            P("dp", None),
        ),
        out_specs=(P(("dp", "head"), None), P("dp", None, None, "head")),
        check_vma=False,
    )
```

profile of v0, /device:TPU:1, one launch (start us, length us, event | category | flops | bytes accessed | tf_op | source)
XLA Modules:
  0.0 179.6 jit_solution(8770833424466064282)
XLA Ops:
  7.2 1.9 %copy.37 = bf16[128,2,16,64]{0,3,2,1:T(8,128)(2,1)} copy(bf16[128,2,16,64]{0,3,2,1:T(8,128)(2,1)} %param.14) | data formatting | bytes 1048576
  9.1 1.2 fusion.49
  10.3 3.7 %collective-permute-start = (bf16[64,3072]{1,0:T(8,128)(2,1)S(1)}, bf16[64,3072]{1,0:T(8,128)(2,1)S(1)}, u32[]{:S(2)}, u32[]{:S(2)}) collective-permute-start(bf16[64,3072]{1,0:T(8,128)(2,1)S(1)} %get-tuple-element.29), channel_id=1, source_target_pairs={{0,8},{1,9},{2,10},{3,11},{4,12},{5,13},{6,14},{7,15},{8,0},{9,1},... | collective-permute-start | bytes 1179656 | tf_op jit(solution)/shard_map/ppermute | solution.py:223
  13.9 0.7 pad_add_fusion.info
  14.6 5.4 %shard_map.104.theirs_ref = bf16[512,512]{1,0:T(8,128)(2,1)} custom-call(s32[3]{0:T(128)} %pad_add_fusion.info, s32[1,4]{1,0:T(1,128)} %lengths.2, bf16[1024,512]{1,0:T(8,128)(2,1)} %q_ref.3, bf16[1024,1024]{1,0:T(8,128)(2,1)} %k_ref.3, bf16[1024,1024]{1,0:T(8,128)(2,1)} %v_ref.3), custom_call_target="tpu_custom_call" | custom-call | flops 805306368 | bytes 2097152 | tf_op jit(solution)/shard_map/pallas_call | solution.py:65
  20.0 1.7 collective-permute-done
  21.7 4.2 %shard_map.105.kept_ref = bf16[512,512]{1,0:T(8,128)(2,1)} custom-call(s32[3]{0:T(128)} %pad_add_fusion.info, s32[1,4]{1,0:T(1,128)} %lengths.2, bf16[1024,512]{1,0:T(8,128)(2,1)} %q_ref.3, bf16[1024,1024]{1,0:T(8,128)(2,1)} %k_ref.3, bf16[1024,1024]{1,0:T(8,128)(2,1)} %v_ref.3), custom_call_target="tpu_custom_call" | custom-call | flops 805306368 | bytes 2097152 | tf_op jit(solution)/shard_map/pallas_call | solution.py:65
  25.9 6.4 %shard_map.106 = bf16[512,4096]{1,0:T(8,128)(2,1)} custom-call(bf16[512,512]{1,0:T(8,128)(2,1)} %shard_map.105.kept_ref, bf16[512,512]{1,0:T(8,128)(2,1)} %shard_map.104.theirs_ref, bf16[512,8192]{1,0:T(8,128)(2,1)} %w_ref.5), custom_call_target="tpu_custom_call" | custom-call | flops 2147483648 | bytes 6291456 | tf_op jit(solution)/shard_map/pallas_call | solution.py:132
  32.5 1.1 dynamic-slice.2
  33.6 5.0 %collective-permute-start.3 = (bf16[128,3072]{1,0:T(8,128)(2,1)S(1)}, bf16[128,3072]{1,0:T(8,128)(2,1)S(1)}, u32[]{:S(2)}, u32[]{:S(2)}) collective-permute-start(bf16[128,3072]{1,0:T(8,128)(2,1)S(1)} %pad_maximum_fusion.3), channel_id=1, source_target_pairs={{0,8},{1,9},{2,10},{3,11},{4,12},{5,13},{6,14},{7,15},{8,0},{9,1},... | collective-permute-start | bytes 2359304 | tf_op jit(solution)/shard_map/ppermute | solution.py:232
  38.7 1.3 collective-permute-start.4
  40.0 1.4 collective-permute-start.5
  41.4 1.6 collective-permute-start.6
  43.1 11.8 %collective-permute-done.3 = bf16[128,3072]{1,0:T(8,128)(2,1)S(1)} collective-permute-done((bf16[128,3072]{1,0:T(8,128)(2,1)S(1)}, bf16[128,3072]{1,0:T(8,128)(2,1)S(1)}, u32[]{:S(2)}, u32[]{:S(2)}) %collective-permute-start.3) | collective-permute-done | bytes 786464 | tf_op jit(solution)/shard_map/ppermute | solution.py:232
  55.0 3.4 %collective-permute-done.6 = bf16[64,3072]{1,0:T(8,128)(2,1)S(1)} collective-permute-done((bf16[64,3072]{1,0:T(8,128)(2,1)S(1)}, bf16[64,3072]{1,0:T(8,128)(2,1)S(1)}, u32[]{:S(2)}, u32[]{:S(2)}) %collective-permute-start.6) | collective-permute-done | bytes 393248 | tf_op jit(solution)/shard_map/ppermute | solution.py:239
  58.3 1.0 collective-permute-start.7
  59.9 6.2 %collective-permute-done.2 = bf16[512,512]{1,0:T(8,128)(2,1)S(1)} collective-permute-done((bf16[512,512]{1,0:T(8,128)(2,1)S(1)}, bf16[512,512]{1,0:T(8,128)(2,1)S(1)}, u32[]{:S(2)}, u32[]{:S(2)}) %collective-permute-start.2) | collective-permute-done | bytes 524320 | tf_op jit(solution)/shard_map/ppermute | solution.py:226
  66.1 2.2 %collective-permute-start.10 = (bf16[256,3072]{1,0:T(8,128)(2,1)S(1)}, bf16[256,3072]{1,0:T(8,128)(2,1)}, u32[]{:S(2)}, u32[]{:S(2)}) collective-permute-start(bf16[256,3072]{1,0:T(8,128)(2,1)S(1)} %pad_maximum_fusion.1.own_ref), channel_id=1, source_target_pairs={{0,16},{16,0},{32,48},{48,32},{64,80},{80,64},{96,112},{112,96},{1... | collective-permute-start | bytes 4718600 | tf_op jit(solution)/shard_map/ppermute | solution.py:242
  68.4 3.9 %collective-permute-start.9 = (bf16[256,3072]{1,0:T(8,128)(2,1)S(1)}, bf16[256,3072]{1,0:T(8,128)(2,1)}, u32[]{:S(2)}, u32[]{:S(2)}) collective-permute-start(bf16[256,3072]{1,0:T(8,128)(2,1)S(1)} %pad_maximum_fusion.own_ref), channel_id=1, source_target_pairs={{0,16},{16,0},{32,48},{48,32},{64,80},{80,64},{96,112},{112,96},{1... | collective-permute-start | bytes 4718600 | tf_op jit(solution)/shard_map/ppermute | solution.py:242
  72.3 2.1 %slice.66 = bf16[64,2,16,64]{0,3,2,1:T(8,128)(2,1)} slice(bf16[128,2,16,64]{0,3,2,1:T(8,128)(2,1)} %copy.37), slice={[64:128], [0:2], [0:16], [0:64]} | slice | bytes 524288 | tf_op jit(solution)/shard_map/slice | solution.py:174
  74.4 1.9 %constant_dynamic-slice_fusion = (bf16[1024,64]{1,0:T(8,128)(2,1)S(1)}, bf16[1024,64]{1,0:T(8,128)(2,1)}) fusion(bf16[1024,1024]{1,0:T(8,128)(2,1)} %v_ref.3, s32[]{:T(128)S(6)} %select_n.165, bf16[1024,1024]{1,0:T(8,128)(2,1)} %k_ref.3), kind=kLoop, calls=%fused_computation.118 | loop fusion | bytes 524292 | tf_op jit(solution)/shard_map/dynamic_slice | solution.py:159
  76.4 2.3 %convolution_convert_fusion.given_ref = bf16[512,512]{1,0:T(8,128)(2,1)} fusion(bf16[512,512]{1,0:T(8,128)(2,1)} %copy-done.8, s32[512]{0:T(512)S(1)} %fusion.30), kind=kOutput, calls=%fused_computation.2 | convolution fusion | flops 268959744 | bytes 1050624 | tf_op jit(solution)/shard_map/dot_general | solution.py:228
  78.7 7.6 %shard_map.107.refs_0_ = bf16[512,6144]{1,0:T(8,128)(2,1)} custom-call(bf16[512,512]{1,0:T(8,128)(2,1)} %shard_map.105.kept_ref, bf16[512,512]{1,0:T(8,128)(2,1)} %convolution_convert_fusion.given_ref, bf16[512,8192]{1,0:T(8,128)(2,1)} %w_ref.5, bf16[256,3072]{1,0:T(8,128)(2,1)} %copy-done, bf16[256,3072]{1,0:T(8,128)(2,1)} %collective-permute-done.10.other_ref), custom_call_target="tpu_custom_call" | custom-call | flops 3221225472 | bytes 9437184 | tf_op jit(solution)/shard_map/pallas_call | solution.py:102
  86.3 7.6 %shard_map.108 = bf16[512,6144]{1,0:T(8,128)(2,1)} custom-call(bf16[512,512]{1,0:T(8,128)(2,1)} %shard_map.105.kept_ref, bf16[512,512]{1,0:T(8,128)(2,1)} %convolution_convert_fusion.given_ref, bf16[512,8192]{1,0:T(8,128)(2,1)} %w_ref.5, bf16[256,3072]{1,0:T(8,128)(2,1)} %copy-done.1, ...), custom_call_target="tpu_custom_call", output_to_operand_aliasing={{}: (5, {})} | custom-call | flops 3221225472 | bytes 9437184 | tf_op jit(solution)/shard_map/pallas_call | solution.py:102
  95.1 1.0 copy-done.3
  96.9 1.6 copy.28
  98.6 0.7 reshape.190
  99.3 0.9 fusion.51
  100.7 0.5 collective-permute-start.11
  101.1 1.2 collective-permute-done.11
  102.7 1.2 fusion.1
  104.2 7.4 %collective-permute-done.12 = bf16[4,2,16384]{2,1,0:T(2,128)(2,1)S(1)} collective-permute-done((bf16[4,2,16384]{2,1,0:T(2,128)(2,1)S(1)}, bf16[4,2,16384]{2,1,0:T(2,128)(2,1)S(1)}, u32[]{:S(2)}, u32[]{:S(2)}) %collective-permute-start.12) | collective-permute-done | bytes 262176 | tf_op jit(solution)/shard_map/ppermute | solution.py:178
  111.6 0.8 fusion.4
  112.7 1.1 collective-permute-start.14
  113.8 1.6 collective-permute-start.15
  115.4 2.4 %dynamic_update_slice.8 = bf16[128,2,16,64]{0,3,2,1:T(8,128)(2,1)S(1)} dynamic-update-slice(bf16[128,2,16,64]{0,3,2,1:T(8,128)(2,1)S(1)} %copy-done.2, bf16[64,2,16,64]{0,3,2,1:T(8,128)(2,1)S(1)} %pad_maximum_fusion.4, s32[]{:T(128)} %constant.173.clone.1, s32[]{:T(128)} %constant.173.clone.1, s32[]{:T(128)} %constant.173.clone.1, s32[]{:T(128)} %constant.173.clone.1) | dynamic-update-slice | bytes 524292 | tf_op jit(solution)/shard_map/dynamic_update_slice | solution.py:195
  117.9 3.4 %collective-permute-done.13 = bf16[2,2,16384]{2,1,0:T(2,128)(2,1)S(1)} collective-permute-done((bf16[2,2,16384]{2,1,0:T(2,128)(2,1)S(1)}, bf16[2,2,16384]{2,1,0:T(2,128)(2,1)S(1)}, u32[]{:S(2)}, u32[]{:S(2)}) %collective-permute-start.13) | collective-permute-done | bytes 131104 | tf_op jit(solution)/shard_map/ppermute | solution.py:179
  121.3 1.0 pad_maximum_fusion.5
  122.3 0.7 reshape.191
  122.9 2.4 %fusion.9 = s32[128]{0:T(128)S(1)} fusion(bf16[128,2,16,64]{3,2,1,0:T(8,128)(2,1)S(1)} %reshape.191), kind=kLoop, calls=%fused_computation.35 | loop fusion | flops 384 | bytes 768 | tf_op jit(solution)/shard_map/convert_element_type | solution.py:183
  125.9 2.4 %compare_reduce_fusion = pred[128]{0:T(512)(128)(4,1)S(1)} fusion(bf16[128,2,16,64]{3,2,1,0:T(8,128)(2,1)S(1)} %reshape.191), kind=kLoop, calls=%fused_computation.26 | loop fusion | flops 256 | bytes 384 | tf_op jit(solution)/shard_map/lt | solution.py:181
  128.4 1.1 copy.30
  130.1 1.0 slice.77
  131.1 2.8 %collective-permute-start.1 = (bf16[64,2048]{1,0:T(8,128)(2,1)S(1)}, bf16[64,2048]{1,0:T(8,128)(2,1)S(1)}, u32[]{:S(2)}, u32[]{:S(2)}) collective-permute-start(bf16[64,2048]{1,0:T(8,128)(2,1)S(1)} %slice.77), channel_id=1, source_target_pairs={{0,8},{1,9},{2,10},{3,11},{4,12},{5,13},{6,14},{7,15},{8,0},{9,1},... | collective-permute-start | bytes 786440 | tf_op jit(solution)/shard_map/ppermute | solution.py:246
  133.9 0.9 convert_select_fusion
  134.8 3.8 %collective-permute-done.1 = bf16[64,2048]{1,0:T(8,128)(2,1)S(1)} collective-permute-done((bf16[64,2048]{1,0:T(8,128)(2,1)S(1)}, bf16[64,2048]{1,0:T(8,128)(2,1)S(1)}, u32[]{:S(2)}, u32[]{:S(2)}) %collective-permute-start.1) | collective-permute-done | bytes 262176 | tf_op jit(solution)/shard_map/ppermute | solution.py:246
  138.7 31.9 %reduce-scatter.5.cloned.1.call-done = bf16[64,6144]{1,0:T(8,128)(2,1)} async-done(((bf16[512,6144]{1,0:T(8,128)(2,1)}), bf16[64,6144]{1,0:T(8,128)(2,1)}) %reduce-scatter.5.cloned.1.call-update) | async-done | bytes 786448 | tf_op jit(solution)/shard_map/reduce_scatter | solution.py:150
  170.6 2.2 %pad_maximum_fusion.2 = bf16[64,8192]{1,0:T(8,128)(2,1)} fusion(bf16[64,6144]{1,0:T(8,128)(2,1)} %reduce-scatter.5.cloned.1.call-done, bf16[64,2048]{1,0:T(8,128)(2,1)S(1)} %add_convert_fusion.1), kind=kLoop, calls=%fused_computation.4 | loop fusion | flops 2097152 | bytes 2097152 | tf_op jit(solution)/shard_map/dynamic_update_slice | solution.py:250
  (67 shorter events, 5.9 us)
Async XLA Ops:
  7.2 122.9 %reduce-scatter.3.cloned.1.call-start = ((), (), s32[]{:S(2)}) async-start(), calls=%async_computation.2 | async-start | bytes 4718592 | tf_op jit(solution)/shard_map/reduce_scatter | solution.py:150
  10.3 11.4 %collective-permute-start = (bf16[64,3072]{1,0:T(8,128)(2,1)S(1)}, bf16[64,3072]{1,0:T(8,128)(2,1)S(1)}, u32[]{:S(2)}, u32[]{:S(2)}) collective-permute-start(bf16[64,3072]{1,0:T(8,128)(2,1)S(1)} %get-tuple-element.29), channel_id=1, source_target_pairs={{0,8},{1,9},{2,10},{3,11},{4,12},{5,13},{6,14},{7,15},{8,0},{9,1},... | collective-permute-start | bytes 1179656 | tf_op jit(solution)/shard_map/ppermute | solution.py:223
  32.4 6.2 %copy-start.4 = (bf16[512,512]{1,0:T(8,128)(2,1)S(1)}, bf16[512,512]{1,0:T(8,128)(2,1)}, u32[]{:S(2)}) copy-start(bf16[512,512]{1,0:T(8,128)(2,1)} %shard_map.104.theirs_ref) | copy-start | bytes 1572868
  32.4 138.2 %reduce-scatter.5.cloned.1.call-start = ((), (), s32[]{:S(2)}) async-start(), calls=%async_computation.3 | async-start | bytes 7077888 | tf_op jit(solution)/shard_map/reduce_scatter | solution.py:150
  33.6 21.3 %collective-permute-start.3 = (bf16[128,3072]{1,0:T(8,128)(2,1)S(1)}, bf16[128,3072]{1,0:T(8,128)(2,1)S(1)}, u32[]{:S(2)}, u32[]{:S(2)}) collective-permute-start(bf16[128,3072]{1,0:T(8,128)(2,1)S(1)} %pad_maximum_fusion.3), channel_id=1, source_target_pairs={{0,8},{1,9},{2,10},{3,11},{4,12},{5,13},{6,14},{7,15},{8,0},{9,1},... | collective-permute-start | bytes 2359304 | tf_op jit(solution)/shard_map/ppermute | solution.py:232
  38.6 27.5 %collective-permute-start.2 = (bf16[512,512]{1,0:T(8,128)(2,1)S(1)}, bf16[512,512]{1,0:T(8,128)(2,1)S(1)}, u32[]{:S(2)}, u32[]{:S(2)}) collective-permute-start(bf16[512,512]{1,0:T(8,128)(2,1)S(1)} %copy-done.4), channel_id=1, source_target_pairs={{0,8},{1,9},{2,10},{3,11},{4,12},{5,13},{6,14},{7,15},{8,0},{9,1},... | collective-permute-start | bytes 1572872 | tf_op jit(solution)/shard_map/ppermute | solution.py:226
  38.7 16.3 %collective-permute-start.4 = (bf16[64,3072]{1,0:T(8,128)(2,1)S(1)}, bf16[64,3072]{1,0:T(8,128)(2,1)S(1)}, u32[]{:S(2)}, u32[]{:S(2)}) collective-permute-start(bf16[64,3072]{1,0:T(8,128)(2,1)S(1)} %collective-permute-done), channel_id=1, source_target_pairs={{0,64},{16,80},{32,96},{48,112},{64,128},{80,144},{96,160},{112,17... | collective-permute-start | bytes 1179656 | tf_op jit(solution)/shard_map/ppermute | solution.py:237
  40.0 15.0 %collective-permute-start.5 = (bf16[64,3072]{1,0:T(8,128)(2,1)S(1)}, bf16[64,3072]{1,0:T(8,128)(2,1)S(1)}, u32[]{:S(2)}, u32[]{:S(2)}) collective-permute-start(bf16[64,3072]{1,0:T(8,128)(2,1)S(1)} %collective-permute-done), channel_id=1, source_target_pairs={{0,192},{16,208},{32,224},{48,240},{64,0},{80,16},{96,32},{112,48}... | collective-permute-start | bytes 1179656 | tf_op jit(solution)/shard_map/ppermute | solution.py:237
  41.4 16.9 %collective-permute-start.6 = (bf16[64,3072]{1,0:T(8,128)(2,1)S(1)}, bf16[64,3072]{1,0:T(8,128)(2,1)S(1)}, u32[]{:S(2)}, u32[]{:S(2)}) collective-permute-start(bf16[64,3072]{1,0:T(8,128)(2,1)S(1)} %collective-permute-done), channel_id=1, source_target_pairs={{0,128},{16,144},{32,160},{48,176},{64,192},{80,208},{96,224},{112... | collective-permute-start | bytes 1179656 | tf_op jit(solution)/shard_map/ppermute | solution.py:239
  58.3 10.0 %collective-permute-start.7 = (bf16[64,3072]{1,0:T(8,128)(2,1)S(1)}, bf16[64,3072]{1,0:T(8,128)(2,1)S(1)}, u32[]{:S(2)}, u32[]{:S(2)}) collective-permute-start(bf16[64,3072]{1,0:T(8,128)(2,1)S(1)} %get-tuple-element.19), channel_id=1, source_target_pairs={{0,192},{16,208},{32,224},{48,240},{64,0},{80,16},{96,32},{112,48}... | collective-permute-start | bytes 1179656 | tf_op jit(solution)/shard_map/ppermute | solution.py:237
  59.4 9.0 %collective-permute-start.8 = (bf16[64,3072]{1,0:T(8,128)(2,1)S(1)}, bf16[64,3072]{1,0:T(8,128)(2,1)S(1)}, u32[]{:S(2)}, u32[]{:S(2)}) collective-permute-start(bf16[64,3072]{1,0:T(8,128)(2,1)S(1)} %get-tuple-element.19), channel_id=1, source_target_pairs={{0,64},{16,80},{32,96},{48,112},{64,128},{80,144},{96,160},{112,17... | collective-permute-start | bytes 1179656 | tf_op jit(solution)/shard_map/ppermute | solution.py:237
  59.9 14.5 %copy-start = (bf16[256,3072]{1,0:T(8,128)(2,1)}, bf16[256,3072]{1,0:T(8,128)(2,1)S(1)}, u32[]{:S(2)}) copy-start(bf16[256,3072]{1,0:T(8,128)(2,1)S(1)} %pad_maximum_fusion.1.own_ref) | copy-start | bytes 4718596
  66.1 2.3 %copy-start.8 = (bf16[512,512]{1,0:T(8,128)(2,1)}, bf16[512,512]{1,0:T(8,128)(2,1)S(1)}, u32[]{:S(2)}) copy-start(bf16[512,512]{1,0:T(8,128)(2,1)S(1)} %collective-permute-done.2) | copy-start | bytes 1572868
  66.1 12.6 %collective-permute-start.10 = (bf16[256,3072]{1,0:T(8,128)(2,1)S(1)}, bf16[256,3072]{1,0:T(8,128)(2,1)}, u32[]{:S(2)}, u32[]{:S(2)}) collective-permute-start(bf16[256,3072]{1,0:T(8,128)(2,1)S(1)} %pad_maximum_fusion.1.own_ref), channel_id=1, source_target_pairs={{0,16},{16,0},{32,48},{48,32},{64,80},{80,64},{96,112},{112,96},{1... | collective-permute-start | bytes 4718600 | tf_op jit(solution)/shard_map/ppermute | solution.py:242
  68.4 17.8 %copy-start.1 = (bf16[256,3072]{1,0:T(8,128)(2,1)}, bf16[256,3072]{1,0:T(8,128)(2,1)S(1)}, u32[]{:S(2)}) copy-start(bf16[256,3072]{1,0:T(8,128)(2,1)S(1)} %pad_maximum_fusion.own_ref) | copy-start | bytes 4718596
  68.4 17.9 %collective-permute-start.9 = (bf16[256,3072]{1,0:T(8,128)(2,1)S(1)}, bf16[256,3072]{1,0:T(8,128)(2,1)}, u32[]{:S(2)}, u32[]{:S(2)}) collective-permute-start(bf16[256,3072]{1,0:T(8,128)(2,1)S(1)} %pad_maximum_fusion.own_ref), channel_id=1, source_target_pairs={{0,16},{16,0},{32,48},{48,32},{64,80},{80,64},{96,112},{112,96},{1... | collective-permute-start | bytes 4718600 | tf_op jit(solution)/shard_map/ppermute | solution.py:242
  86.3 7.7 %copy-start.5 = (bf16[1024,64]{1,0:T(8,128)(2,1)S(1)}, bf16[1024,64]{1,0:T(8,128)(2,1)}, u32[]{:S(2)}) copy-start(bf16[1024,64]{1,0:T(8,128)(2,1)} %get-tuple-element.25) | copy-start | bytes 393220
  86.3 8.2 %copy-start.7 = (s32[64,1]{0,1:T(1,128)S(1)}, s32[64,1]{0,1:T(1,128)}, u32[]{:S(2)}) copy-start(s32[64,1]{0,1:T(1,128)} %param.16) | copy-start | bytes 772
  86.3 8.4 %copy-start.9 = (s32[64]{0:T(128)S(1)}, s32[64]{0:T(128)}, u32[]{:S(2)}) copy-start(s32[64]{0:T(128)} %param.15) | copy-start | bytes 772
  95.0 1.0 copy-start.3
  100.2 15.2 %copy-start.2 = (bf16[128,2,16,64]{0,3,2,1:T(8,128)(2,1)S(1)}, bf16[128,2,16,64]{0,3,2,1:T(8,128)(2,1)}, u32[]{:S(2)}) copy-start(bf16[128,2,16,64]{0,3,2,1:T(8,128)(2,1)} %copy.37) | copy-start | bytes 1572868
  100.7 1.7 collective-permute-start.11
  102.3 15.5 %copy-start.10 = (s32[1,128]{1,0:T(1,128)S(1)}, s32[1,128]{1,0:T(1,128)}, u32[]{:S(2)}) copy-start(s32[1,128]{1,0:T(1,128)} %param.17) | copy-start | bytes 1540
  103.9 7.7 %collective-permute-start.12 = (bf16[4,2,16384]{2,1,0:T(2,128)(2,1)S(1)}, bf16[4,2,16384]{2,1,0:T(2,128)(2,1)S(1)}, u32[]{:S(2)}, u32[]{:S(2)}) collective-permute-start(bf16[4,2,16384]{2,1,0:T(2,128)(2,1)S(1)} %get-tuple-element.31), channel_id=1, source_target_pairs={{0,32},{16,48},{32,0},{48,16},{64,96},{80,112},{96,64},{112,80},{1... | collective-permute-start | bytes 786440 | tf_op jit(solution)/shard_map/ppermute | solution.py:178
  112.4 8.9 %collective-permute-start.13 = (bf16[2,2,16384]{2,1,0:T(2,128)(2,1)S(1)}, bf16[2,2,16384]{2,1,0:T(2,128)(2,1)S(1)}, u32[]{:S(2)}, u32[]{:S(2)}) collective-permute-start(bf16[2,2,16384]{2,1,0:T(2,128)(2,1)S(1)} %get-tuple-element.35), channel_id=1, source_target_pairs={{0,64},{16,80},{32,96},{48,112},{64,128},{80,144},{96,160},{112,17... | collective-permute-start | bytes 393224 | tf_op jit(solution)/shard_map/ppermute | solution.py:179
  112.7 8.6 %collective-permute-start.14 = (bf16[2,2,16384]{2,1,0:T(2,128)(2,1)S(1)}, bf16[2,2,16384]{2,1,0:T(2,128)(2,1)S(1)}, u32[]{:S(2)}, u32[]{:S(2)}) collective-permute-start(bf16[2,2,16384]{2,1,0:T(2,128)(2,1)S(1)} %get-tuple-element.37), channel_id=1, source_target_pairs={{0,128},{16,144},{32,160},{48,176},{64,192},{80,208},{96,224},{112... | collective-permute-start | bytes 393224 | tf_op jit(solution)/shard_map/ppermute | solution.py:179
  113.8 7.5 %collective-permute-start.15 = (bf16[2,2,16384]{2,1,0:T(2,128)(2,1)S(1)}, bf16[2,2,16384]{2,1,0:T(2,128)(2,1)S(1)}, u32[]{:S(2)}, u32[]{:S(2)}) collective-permute-start(bf16[2,2,16384]{2,1,0:T(2,128)(2,1)S(1)} %get-tuple-element.36), channel_id=1, source_target_pairs={{0,192},{16,208},{32,224},{48,240},{64,0},{80,16},{96,32},{112,48}... | collective-permute-start | bytes 393224 | tf_op jit(solution)/shard_map/ppermute | solution.py:179
  130.1 8.5 %copy-start.6 = (bf16[64,4096]{1,0:T(8,128)(2,1)S(1)}, bf16[64,4096]{1,0:T(8,128)(2,1)}, u32[]{:S(2)}) copy-start(bf16[64,4096]{1,0:T(8,128)(2,1)} %reduce-scatter.3.cloned.1.call-done) | copy-start | bytes 1572868
  131.1 7.4 %collective-permute-start.1 = (bf16[64,2048]{1,0:T(8,128)(2,1)S(1)}, bf16[64,2048]{1,0:T(8,128)(2,1)S(1)}, u32[]{:S(2)}, u32[]{:S(2)}) collective-permute-start(bf16[64,2048]{1,0:T(8,128)(2,1)S(1)} %slice.77), channel_id=1, source_target_pairs={{0,8},{1,9},{2,10},{3,11},{4,12},{5,13},{6,14},{7,15},{8,0},{9,1},... | collective-permute-start | bytes 786440 | tf_op jit(solution)/shard_map/ppermute | solution.py:246
Sparse Core Ops, SparseCore 0:
  32.5 61.3 reduce-scatter.2
  96.4 74.1 reduce-scatter.4
where the time goes:
time: 180 us
  waiting for transfers between devices  70.9 us (39%)
  Pallas kernels  31.2 us (17%)
  starting transfers between devices  27.2 us (15%)
  local copies, waits for them, and re-layouts  19.3 us (11%)
  between operations  14.4 us (8%)
  other arithmetic  13 us (7%)
  matrix products  3.53 us (2%)
    reduce_scatter x2, waiting for transfers between devices, sum_over_z(): lax.psum_scatter(part, 'head', scatter_dimension=0, axis_index_groups=Z_G...  31.9 us
    pallas_call x2, Pallas kernels, project(): pl.pallas_call(project_kernel, grid=((last - first) // TILE,), in_specs=[...  15.2 us
    ppermute x1, waiting for transfers between devices, on_device(): got.append(lax.ppermute(after(both, got[0]), 'head', X_SWAP))  11.8 us
    pallas_call x2, Pallas kernels, attend_half(): pl.pallas_call(functools.partial(attend_kernel, side), grid_spec=pltpu.Pr...  9.61 us
    ppermute x1, waiting for transfers between devices, migrate(): b = jnp.stack([b[:, 0], lax.ppermute(b[:, 1], 'dp', LO_SWAP)], axis=1)  7.42 us
    pallas_call x1, Pallas kernels, project_first(): pl.pallas_call(project_first_kernel, grid=(2, tiles), in_specs=[pl.BlockS...  6.44 us
    ppermute x1, waiting for transfers between devices, on_device(): came = lax.ppermute(theirs, 'head', X_SWAP)  6.19 us
    ppermute x2, starting transfers between devices, on_device(): sides.append((own, lax.ppermute(own, 'dp', CORE_SWAP)))  6.05 us
  transfers between devices with their start and end apart: 18, of which 9 were waited for; matrix products, arithmetic and copies ran while one was open for 16% of the time, Pallas kernels for 11%

commit v1 on v0

--- a/solution.py
+++ b/solution.py
@@ -156,7 +156,9 @@
     at = lax.axis_index("head") * width
     me = lax.axis_index("dp")
     y, low = me // 4, me % 4
-    rows = [after(lax.dynamic_slice_in_dim(a, at, width, 1), targets) for a in (key_rows, value_rows)]
+    at, half = after(jnp.stack([at, jnp.int32(written)]), targets)
+    rows = [lax.dynamic_slice_in_dim(a, at, width, 1) for a in (key_rows, value_rows)]
+    unwritten = lax.dynamic_slice_in_dim(cache_pool, half, pool - written, 0)
     span = jnp.stack([a.reshape(written, BT, width) for a in rows], axis=1)
     r = jnp.arange(16, dtype=jnp.int32)
     target_place = ((targets // 4 - y) % NY) * 4 + ((targets % 4) ^ low)
@@ -171,7 +173,7 @@
     pick = jnp.dot(picks, blocks, preferred_element_type=F32).astype(BF)
     empty = 1.0 - jnp.sum(pick.astype(F32), axis=1)
     sending = jnp.einsum("sb,bktf->sktf", pick[:, :written], span, preferred_element_type=F32)
-    sending = sending + jnp.einsum("sb,bktf->sktf", pick[:, written:], cache_pool[written:], preferred_element_type=F32)
+    sending = sending + jnp.einsum("sb,bktf->sktf", pick[:, written:], unwritten, preferred_element_type=F32)
     sending = (sending + 256.0 * empty[:, None, None, None]).astype(BF)
     b = sending.reshape(NY, 2, 2, 8 * 2 * BT * width)
     b = jnp.stack([b[:, :, 0], lax.ppermute(b[:, :, 1], "dp", CORE_SWAP)], axis=2)
@@ -192,7 +194,7 @@
     fresh = jnp.einsum(
         "sktf,sb->bktf", jnp.where(valid.reshape(128, 1, 1, 1), arrived, 0), hits.astype(BF), preferred_element_type=F32
     ).astype(BF)
-    sectioned = lax.dynamic_update_slice_in_dim(cache_pool, span, 0, 0)
+    sectioned = jnp.concatenate([span, unwritten], axis=0)
     return jnp.where(taken[:, None, None, None], fresh, sectioned)
 
 
@@ -224,9 +226,9 @@
     opposite = lax.dynamic_slice_in_dim(after(out_weight, got[0]), ((y + 2) % NY * 2 + core) * eighth, eighth, 0)
     theirs = attend_half(0, info, prompt_lengths, query_rows, key_rows, value_rows)
     came = lax.ppermute(theirs, "head", X_SWAP)
-    kept = attend_half(1, info, after(prompt_lengths, theirs, got[0]), query_rows, key_rows, value_rows)
+    kept = attend_half(1, info, after(prompt_lengths, theirs), query_rows, key_rows, value_rows)
     given = jnp.dot(came, order, preferred_element_type=F32).astype(BF)
-    part = project_first(kept, theirs, out_weight, FIRST)
+    part = project_first(kept, after(theirs, got[0]), out_weight, FIRST)
     firsts = sum_over_z(part).reshape(count // NZ, 2 * FIRST)
     both = jnp.concatenate([slab[:, slice(*GROUPS[1])], opposite[:, slice(*GROUPS[1])]], axis=0)
     got.append(lax.ppermute(after(both, got[0]), "head", X_SWAP))

time: 180 us -> 173 us (0.961)
  local copies, waits for them, and re-layouts: 19.3 us -> 13.1 us
  between operations: 14.4 us -> 18.4 us
  starting transfers between devices: 27.2 us -> 23.5 us
  waiting for transfers between devices: 70.9 us -> 67.9 us
    reduce_scatter x2, waiting for transfers between devices: 31.9 us -> 24.5 us  [sum_over_z(): lax.psum_scatter(part, 'head', scatter_dimension=0, axis_index_groups=Z_G...]
    ppermute x4, waiting for transfers between devices: 0.01 us -> 7.06 us  [on_device(): near, far = (lax.ppermute(piece, 'dp', y_shift(k)) for k in (1, -1))]
    ppermute x1, starting transfers between devices: 4.97 us -> 1.34 us  [on_device(): got.append(lax.ppermute(after(both, got[0]), 'head', X_SWAP))]
    ppermute x1, waiting for transfers between devices: 3.38 us -> 0.01 us  [on_device(): across = lax.ppermute(piece, 'dp', y_shift(2))]
    unnamed x24 -> x19, local copies, waits for them, and re-layouts: 3.35 us -> 0.46 us
    ppermute x2, starting transfers between devices: 6.05 us -> 3.38 us  [on_device(): sides.append((own, lax.ppermute(own, 'dp', CORE_SWAP)))]
    dynamic_update_slice x1 -> x0, local copies, waits for them, and re-layouts: 2.37 us -> none  [migrate(): sectioned = lax.dynamic_update_slice_in_dim(cache_pool, span, 0, 0)]
    ppermute x1, waiting for transfers between devices: 6.19 us -> 3.92 us  [on_device(): came = lax.ppermute(theirs, 'head', X_SWAP)]
  transfers between devices with their start and end apart: 18 -> 18, of which waited for: 9 -> 11; matrix products, arithmetic and copies ran while one was open for 16% -> 16% of each run, Pallas kernels for 11% -> 14%
where the time goes in v1:
time: 173 us; the launch traced here: 172 us
  waiting for transfers between devices  67.9 us (39%)
  Pallas kernels  31.1 us (18%)
  starting transfers between devices  23.5 us (14%)
  between operations  18.4 us (11%)
  other arithmetic  14.5 us (8%)
  local copies, waits for them, and re-layouts  13.1 us (8%)
  matrix products  3.53 us (2%)
    reduce_scatter x2, waiting for transfers between devices, sum_over_z(): lax.psum_scatter(part, 'head', scatter_dimension=0, axis_index_groups=Z_G...  24.5 us
    pallas_call x2, Pallas kernels, project(): pl.pallas_call(project_kernel, grid=((last - first) // TILE,), in_specs=[...  15.1 us
    ppermute x1, waiting for transfers between devices, on_device(): got.append(lax.ppermute(after(both, got[0]), 'head', X_SWAP))  12.2 us
    pallas_call x2, Pallas kernels, attend_half(): pl.pallas_call(functools.partial(attend_kernel, side), grid_spec=pltpu.Pr...  9.6 us
    ppermute x1, waiting for transfers between devices, migrate(): b = jnp.stack([b[:, 0], lax.ppermute(b[:, 1], 'dp', LO_SWAP)], axis=1)  7.58 us
    ppermute x4, waiting for transfers between devices, on_device(): near, far = (lax.ppermute(piece, 'dp', y_shift(k)) for k in (1, -1))  7.06 us
    pallas_call x1, Pallas kernels, project_first(): pl.pallas_call(project_first_kernel, grid=(2, tiles), in_specs=[pl.BlockS...  6.39 us
    ppermute x1, waiting for transfers between devices, on_device(): swapped = lax.ppermute(firsts[:, FIRST:], 'head', X_SWAP)  5.51 us
  transfers between devices with their start and end apart: 18, of which 11 were waited for; matrix products, arithmetic and copies ran while one was open for 16% of the time, Pallas kernels for 14%

profile of v1, /device:TPU:1, one launch (start us, length us, event | category | flops | bytes accessed | tf_op | source)
XLA Modules:
  0.0 172.0 jit_solution(9784521955346099506)
XLA Ops:
  7.3 1.2 fusion.49
  8.5 3.7 %collective-permute-start = (bf16[64,3072]{1,0:T(8,128)(2,1)S(1)}, bf16[64,3072]{1,0:T(8,128)(2,1)S(1)}, u32[]{:S(2)}, u32[]{:S(2)}) collective-permute-start(bf16[64,3072]{1,0:T(8,128)(2,1)S(1)} %get-tuple-element.29), channel_id=1, source_target_pairs={{0,8},{1,9},{2,10},{3,11},{4,12},{5,13},{6,14},{7,15},{8,0},{9,1},... | collective-permute-start | bytes 1179656 | tf_op jit(solution)/shard_map/ppermute | solution.py:225
  12.8 5.4 %shard_map.104.theirs_ref = bf16[512,512]{1,0:T(8,128)(2,1)} custom-call(s32[3]{0:T(128)} %pad_add_fusion.info, s32[1,4]{1,0:T(1,128)} %lengths.2, bf16[1024,512]{1,0:T(8,128)(2,1)} %q_ref.3, bf16[1024,1024]{1,0:T(8,128)(2,1)} %k_ref.3, bf16[1024,1024]{1,0:T(8,128)(2,1)} %v_ref.3), custom_call_target="tpu_custom_call" | custom-call | flops 805306368 | bytes 2097152 | tf_op jit(solution)/shard_map/pallas_call | solution.py:65
  18.1 4.2 %shard_map.105.kept_ref = bf16[512,512]{1,0:T(8,128)(2,1)} custom-call(s32[3]{0:T(128)} %pad_add_fusion.info, s32[1,4]{1,0:T(1,128)} %lengths.2, bf16[1024,512]{1,0:T(8,128)(2,1)} %q_ref.3, bf16[1024,1024]{1,0:T(8,128)(2,1)} %k_ref.3, bf16[1024,1024]{1,0:T(8,128)(2,1)} %v_ref.3), custom_call_target="tpu_custom_call" | custom-call | flops 805306368 | bytes 2097152 | tf_op jit(solution)/shard_map/pallas_call | solution.py:65
  22.4 6.4 %shard_map.106 = bf16[512,4096]{1,0:T(8,128)(2,1)} custom-call(bf16[512,512]{1,0:T(8,128)(2,1)} %shard_map.105.kept_ref, bf16[512,512]{1,0:T(8,128)(2,1)} %shard_map.104.theirs_ref, bf16[512,8192]{1,0:T(8,128)(2,1)} %w_ref.5), custom_call_target="tpu_custom_call" | custom-call | flops 2147483648 | bytes 6291456 | tf_op jit(solution)/shard_map/pallas_call | solution.py:132
  28.9 1.1 dynamic-slice.2
  30.0 1.3 collective-permute-start.3
  31.3 1.7 collective-permute-start.2
  33.1 2.9 %collective-permute-start.6 = (bf16[64,3072]{1,0:T(8,128)(2,1)S(1)}, bf16[64,3072]{1,0:T(8,128)(2,1)S(1)}, u32[]{:S(2)}, u32[]{:S(2)}) collective-permute-start(bf16[64,3072]{1,0:T(8,128)(2,1)S(1)} %collective-permute-done), channel_id=1, source_target_pairs={{0,128},{16,144},{32,160},{48,176},{64,192},{80,208},{96,224},{112... | collective-permute-start | bytes 1179656 | tf_op jit(solution)/shard_map/ppermute | solution.py:241
  36.0 0.8 collective-permute-start.5
  36.8 0.7 collective-permute-start.4
  37.4 12.2 %collective-permute-done.3 = bf16[128,3072]{1,0:T(8,128)(2,1)S(1)} collective-permute-done((bf16[128,3072]{1,0:T(8,128)(2,1)S(1)}, bf16[128,3072]{1,0:T(8,128)(2,1)S(1)}, u32[]{:S(2)}, u32[]{:S(2)}) %collective-permute-start.3) | collective-permute-done | bytes 786464 | tf_op jit(solution)/shard_map/ppermute | solution.py:234
  49.7 3.6 %collective-permute-done.5 = bf16[64,3072]{1,0:T(8,128)(2,1)S(1)} collective-permute-done((bf16[64,3072]{1,0:T(8,128)(2,1)S(1)}, bf16[64,3072]{1,0:T(8,128)(2,1)S(1)}, u32[]{:S(2)}, u32[]{:S(2)}) %collective-permute-start.5) | collective-permute-done | bytes 393248 | tf_op jit(solution)/shard_map/ppermute | solution.py:239
  53.4 0.8 collective-permute-done.4
  54.1 1.3 collective-permute-start.8
  55.4 1.4 collective-permute-start.7
  57.0 3.9 %collective-permute-done.2 = bf16[512,512]{1,0:T(8,128)(2,1)S(1)} collective-permute-done((bf16[512,512]{1,0:T(8,128)(2,1)S(1)}, bf16[512,512]{1,0:T(8,128)(2,1)S(1)}, u32[]{:S(2)}, u32[]{:S(2)}) %collective-permute-start.2) | collective-permute-done | bytes 524320 | tf_op jit(solution)/shard_map/ppermute | solution.py:228
  60.9 1.9 %collective-permute-start.10 = (bf16[256,3072]{1,0:T(8,128)(2,1)S(1)}, bf16[256,3072]{1,0:T(8,128)(2,1)}, u32[]{:S(2)}, u32[]{:S(2)}) collective-permute-start(bf16[256,3072]{1,0:T(8,128)(2,1)S(1)} %pad_maximum_fusion.1.own_ref), channel_id=1, source_target_pairs={{0,16},{16,0},{32,48},{48,32},{64,80},{80,64},{96,112},{112,96},{1... | collective-permute-start | bytes 4718600 | tf_op jit(solution)/shard_map/ppermute | solution.py:244
  62.8 2.7 %collective-permute-done.8 = bf16[64,3072]{1,0:T(8,128)(2,1)S(1)} collective-permute-done((bf16[64,3072]{1,0:T(8,128)(2,1)S(1)}, bf16[64,3072]{1,0:T(8,128)(2,1)S(1)}, u32[]{:S(2)}, u32[]{:S(2)}) %collective-permute-start.8) | collective-permute-done | bytes 393248 | tf_op jit(solution)/shard_map/ppermute | solution.py:239
  65.5 1.3 pad_maximum_fusion.own_ref
  66.7 1.5 collective-permute-start.9
  68.3 1.3 convolution_convert_fusion.given_ref
  69.6 7.5 %shard_map.107.refs_0_ = bf16[512,6144]{1,0:T(8,128)(2,1)} custom-call(bf16[512,512]{1,0:T(8,128)(2,1)} %shard_map.105.kept_ref, bf16[512,512]{1,0:T(8,128)(2,1)} %convolution_convert_fusion.given_ref, bf16[512,8192]{1,0:T(8,128)(2,1)} %w_ref.5, bf16[256,3072]{1,0:T(8,128)(2,1)} %copy-done.1, bf16[256,3072]{1,0:T(8,128)(2,1)} %collective-permute-done.10.other_ref), custom_call_target="tpu_custom_call" | custom-call | flops 3221225472 | bytes 9437184 | tf_op jit(solution)/shard_map/pallas_call | solution.py:102
  77.2 7.6 %shard_map.108 = bf16[512,6144]{1,0:T(8,128)(2,1)} custom-call(bf16[512,512]{1,0:T(8,128)(2,1)} %shard_map.105.kept_ref, bf16[512,512]{1,0:T(8,128)(2,1)} %convolution_convert_fusion.given_ref, bf16[512,8192]{1,0:T(8,128)(2,1)} %w_ref.5, bf16[256,3072]{1,0:T(8,128)(2,1)} %pad_maximum_fusion.own_ref, ...), custom_call_target="tpu_custom_call", output_to_operand_aliasing={{}: (5, {})} | custom-call | flops 3221225472 | bytes 9437184 | tf_op jit(solution)/shard_map/pallas_call | solution.py:102
  89.3 1.4 constant_dynamic-slice_fusion.1
  93.1 1.6 copy.28
  94.7 0.7 reshape.190
  95.4 0.9 fusion.51
  96.9 1.5 collective-permute-done.11
  98.8 1.2 fusion.1
  100.4 7.6 %collective-permute-done.12 = bf16[4,2,16384]{2,1,0:T(2,128)(2,1)S(1)} collective-permute-done((bf16[4,2,16384]{2,1,0:T(2,128)(2,1)S(1)}, bf16[4,2,16384]{2,1,0:T(2,128)(2,1)S(1)}, u32[]{:S(2)}, u32[]{:S(2)}) %collective-permute-start.12) | collective-permute-done | bytes 262176 | tf_op jit(solution)/shard_map/ppermute | solution.py:180
  108.0 0.8 fusion.4
  108.7 1.6 collective-permute-start.13
  110.3 1.5 collective-permute-start.15
  111.8 1.3 collective-permute-start.14
  113.3 1.3 collective-permute-done.13
  114.6 4.2 %collective-permute-done.14 = bf16[2,2,16384]{2,1,0:T(2,128)(2,1)S(1)} collective-permute-done((bf16[2,2,16384]{2,1,0:T(2,128)(2,1)S(1)}, bf16[2,2,16384]{2,1,0:T(2,128)(2,1)S(1)}, u32[]{:S(2)}, u32[]{:S(2)}) %collective-permute-start.14) | collective-permute-done | bytes 131104 | tf_op jit(solution)/shard_map/ppermute | solution.py:181
  118.8 1.0 pad_maximum_fusion.5
  120.4 2.4 %compare_reduce_fusion = pred[128]{0:T(512)(128)(4,1)S(1)} fusion(bf16[128,2,16,64]{3,2,1,0:T(8,128)(2,1)S(1)} %reshape.191), kind=kLoop, calls=%fused_computation.26 | loop fusion | flops 256 | bytes 384 | tf_op jit(solution)/shard_map/lt | solution.py:183
  123.0 1.9 %copy.30 = bf16[128,2,16,64]{0,3,2,1:T(8,128)(2,1)} copy(bf16[128,2,16,64]{3,2,1,0:T(8,128)(2,1)S(1)} %broadcast_select_fusion) | data formatting | bytes 1048576 | tf_op jit(solution)/shard_map/jit(_where)/select_n | solution.py:195
  124.8 2.4 %fusion.9 = s32[128]{0:T(128)S(1)} fusion(bf16[128,2,16,64]{3,2,1,0:T(8,128)(2,1)S(1)} %reshape.191), kind=kLoop, calls=%fused_computation.35 | loop fusion | flops 384 | bytes 768 | tf_op jit(solution)/shard_map/convert_element_type | solution.py:185
  127.9 1.4 fusion.10
  129.4 1.0 slice.73
  130.4 1.3 collective-permute-start.1
  131.7 1.1 maximum_select_fusion
  132.9 5.5 %collective-permute-done.1 = bf16[64,2048]{1,0:T(8,128)(2,1)S(1)} collective-permute-done((bf16[64,2048]{1,0:T(8,128)(2,1)S(1)}, bf16[64,2048]{1,0:T(8,128)(2,1)S(1)}, u32[]{:S(2)}, u32[]{:S(2)}) %collective-permute-start.1) | collective-permute-done | bytes 262176 | tf_op jit(solution)/shard_map/ppermute | solution.py:248
  138.4 24.5 %reduce-scatter.5.cloned.1.call-done = bf16[64,6144]{1,0:T(8,128)(2,1)} async-done(((bf16[512,6144]{1,0:T(8,128)(2,1)}), bf16[64,6144]{1,0:T(8,128)(2,1)}) %reduce-scatter.5.cloned.1.call-update) | async-done | bytes 786448 | tf_op jit(solution)/shard_map/reduce_scatter | solution.py:150
  162.9 2.2 %pad_maximum_fusion.2 = bf16[64,8192]{1,0:T(8,128)(2,1)} fusion(bf16[64,6144]{1,0:T(8,128)(2,1)} %reduce-scatter.5.cloned.1.call-done, bf16[64,2048]{1,0:T(8,128)(2,1)S(1)} %add_convert_fusion.1), kind=kLoop, calls=%fused_computation.4 | loop fusion | flops 2097152 | bytes 2097152 | tf_op jit(solution)/shard_map/dynamic_update_slice | solution.py:252
  (63 shorter events, 6.9 us)
Async XLA Ops:
  7.2 85.2 %copy-start = (bf16[128,2,16,64]{0,3,2,1:T(8,128)(2,1)S(1)}, bf16[128,2,16,64]{0,3,2,1:T(8,128)(2,1)}, u32[]{:S(2)}) copy-start(bf16[128,2,16,64]{0,3,2,1:T(8,128)(2,1)} %param.14) | copy-start | bytes 1572868
  7.2 122.2 %reduce-scatter.3.cloned.1.call-start = ((), (), s32[]{:S(2)}) async-start(), calls=%async_computation.2 | async-start | bytes 4718592 | tf_op jit(solution)/shard_map/reduce_scatter | solution.py:150
  8.5 13.9 %collective-permute-start = (bf16[64,3072]{1,0:T(8,128)(2,1)S(1)}, bf16[64,3072]{1,0:T(8,128)(2,1)S(1)}, u32[]{:S(2)}, u32[]{:S(2)}) collective-permute-start(bf16[64,3072]{1,0:T(8,128)(2,1)S(1)} %get-tuple-element.29), channel_id=1, source_target_pairs={{0,8},{1,9},{2,10},{3,11},{4,12},{5,13},{6,14},{7,15},{8,0},{9,1},... | collective-permute-start | bytes 1179656 | tf_op jit(solution)/shard_map/ppermute | solution.py:225
  28.8 2.6 %copy-start.4 = (bf16[512,512]{1,0:T(8,128)(2,1)S(1)}, bf16[512,512]{1,0:T(8,128)(2,1)}, u32[]{:S(2)}) copy-start(bf16[512,512]{1,0:T(8,128)(2,1)} %shard_map.104.theirs_ref) | copy-start | bytes 1572868
  28.8 134.2 %reduce-scatter.5.cloned.1.call-start = ((), (), s32[]{:S(2)}) async-start(), calls=%async_computation.3 | async-start | bytes 7077888 | tf_op jit(solution)/shard_map/reduce_scatter | solution.py:150
  30.0 19.7 %collective-permute-start.3 = (bf16[128,3072]{1,0:T(8,128)(2,1)S(1)}, bf16[128,3072]{1,0:T(8,128)(2,1)S(1)}, u32[]{:S(2)}, u32[]{:S(2)}) collective-permute-start(bf16[128,3072]{1,0:T(8,128)(2,1)S(1)} %pad_maximum_fusion.3), channel_id=1, source_target_pairs={{0,8},{1,9},{2,10},{3,11},{4,12},{5,13},{6,14},{7,15},{8,0},{9,1},... | collective-permute-start | bytes 2359304 | tf_op jit(solution)/shard_map/ppermute | solution.py:234
  31.3 29.6 %collective-permute-start.2 = (bf16[512,512]{1,0:T(8,128)(2,1)S(1)}, bf16[512,512]{1,0:T(8,128)(2,1)S(1)}, u32[]{:S(2)}, u32[]{:S(2)}) collective-permute-start(bf16[512,512]{1,0:T(8,128)(2,1)S(1)} %copy-done.4), channel_id=1, source_target_pairs={{0,8},{1,9},{2,10},{3,11},{4,12},{5,13},{6,14},{7,15},{8,0},{9,1},... | collective-permute-start | bytes 1572872 | tf_op jit(solution)/shard_map/ppermute | solution.py:228
  33.1 16.7 %collective-permute-start.6 = (bf16[64,3072]{1,0:T(8,128)(2,1)S(1)}, bf16[64,3072]{1,0:T(8,128)(2,1)S(1)}, u32[]{:S(2)}, u32[]{:S(2)}) collective-permute-start(bf16[64,3072]{1,0:T(8,128)(2,1)S(1)} %collective-permute-done), channel_id=1, source_target_pairs={{0,128},{16,144},{32,160},{48,176},{64,192},{80,208},{96,224},{112... | collective-permute-start | bytes 1179656 | tf_op jit(solution)/shard_map/ppermute | solution.py:241
  36.0 17.4 %collective-permute-start.5 = (bf16[64,3072]{1,0:T(8,128)(2,1)S(1)}, bf16[64,3072]{1,0:T(8,128)(2,1)S(1)}, u32[]{:S(2)}, u32[]{:S(2)}) collective-permute-start(bf16[64,3072]{1,0:T(8,128)(2,1)S(1)} %collective-permute-done), channel_id=1, source_target_pairs={{0,192},{16,208},{32,224},{48,240},{64,0},{80,16},{96,32},{112,48}... | collective-permute-start | bytes 1179656 | tf_op jit(solution)/shard_map/ppermute | solution.py:239
  36.8 17.4 %collective-permute-start.4 = (bf16[64,3072]{1,0:T(8,128)(2,1)S(1)}, bf16[64,3072]{1,0:T(8,128)(2,1)S(1)}, u32[]{:S(2)}, u32[]{:S(2)}) collective-permute-start(bf16[64,3072]{1,0:T(8,128)(2,1)S(1)} %collective-permute-done), channel_id=1, source_target_pairs={{0,64},{16,80},{32,96},{48,112},{64,128},{80,144},{96,160},{112,17... | collective-permute-start | bytes 1179656 | tf_op jit(solution)/shard_map/ppermute | solution.py:239
  54.1 11.3 %collective-permute-start.8 = (bf16[64,3072]{1,0:T(8,128)(2,1)S(1)}, bf16[64,3072]{1,0:T(8,128)(2,1)S(1)}, u32[]{:S(2)}, u32[]{:S(2)}) collective-permute-start(bf16[64,3072]{1,0:T(8,128)(2,1)S(1)} %get-tuple-element.20), channel_id=1, source_target_pairs={{0,64},{16,80},{32,96},{48,112},{64,128},{80,144},{96,160},{112,17... | collective-permute-start | bytes 1179656 | tf_op jit(solution)/shard_map/ppermute | solution.py:239
  55.4 10.0 %collective-permute-start.7 = (bf16[64,3072]{1,0:T(8,128)(2,1)S(1)}, bf16[64,3072]{1,0:T(8,128)(2,1)S(1)}, u32[]{:S(2)}, u32[]{:S(2)}) collective-permute-start(bf16[64,3072]{1,0:T(8,128)(2,1)S(1)} %get-tuple-element.20), channel_id=1, source_target_pairs={{0,192},{16,208},{32,224},{48,240},{64,0},{80,16},{96,32},{112,48}... | collective-permute-start | bytes 1179656 | tf_op jit(solution)/shard_map/ppermute | solution.py:239
  57.0 12.6 %copy-start.1 = (bf16[256,3072]{1,0:T(8,128)(2,1)}, bf16[256,3072]{1,0:T(8,128)(2,1)S(1)}, u32[]{:S(2)}) copy-start(bf16[256,3072]{1,0:T(8,128)(2,1)S(1)} %pad_maximum_fusion.1.own_ref) | copy-start | bytes 4718596
  60.9 8.7 %collective-permute-start.10 = (bf16[256,3072]{1,0:T(8,128)(2,1)S(1)}, bf16[256,3072]{1,0:T(8,128)(2,1)}, u32[]{:S(2)}, u32[]{:S(2)}) collective-permute-start(bf16[256,3072]{1,0:T(8,128)(2,1)S(1)} %pad_maximum_fusion.1.own_ref), channel_id=1, source_target_pairs={{0,16},{16,0},{32,48},{48,32},{64,80},{80,64},{96,112},{112,96},{1... | collective-permute-start | bytes 4718600 | tf_op jit(solution)/shard_map/ppermute | solution.py:244
  66.7 10.4 %collective-permute-start.9 = (bf16[256,3072]{1,0:T(8,128)(2,1)}, bf16[256,3072]{1,0:T(8,128)(2,1)}, u32[]{:S(2)}, u32[]{:S(2)}) collective-permute-start(bf16[256,3072]{1,0:T(8,128)(2,1)} %pad_maximum_fusion.own_ref), channel_id=1, source_target_pairs={{0,16},{16,0},{32,48},{48,32},{64,80},{80,64},{96,112},{112,96},{1... | collective-permute-start | bytes 4718600 | tf_op jit(solution)/shard_map/ppermute | solution.py:244
  77.2 7.6 %copy-start.6 = (s32[64,1]{0,1:T(1,128)S(1)}, s32[64,1]{0,1:T(1,128)}, u32[]{:S(2)}) copy-start(s32[64,1]{0,1:T(1,128)} %param.16) | copy-start | bytes 772
  84.9 3.4 %copy-start.7 = (s32[64]{0:T(128)S(1)}, s32[64]{0:T(128)}, u32[]{:S(2)}) copy-start(s32[64]{0:T(128)} %param.15) | copy-start | bytes 772
  91.3 1.6 copy-start.2
  96.3 16.8 %copy-start.8 = (s32[1,128]{1,0:T(1,128)S(1)}, s32[1,128]{1,0:T(1,128)}, u32[]{:S(2)}) copy-start(s32[1,128]{1,0:T(1,128)} %param.17) | copy-start | bytes 1540
  96.8 1.6 collective-permute-start.11
  100.0 8.0 %collective-permute-start.12 = (bf16[4,2,16384]{2,1,0:T(2,128)(2,1)S(1)}, bf16[4,2,16384]{2,1,0:T(2,128)(2,1)S(1)}, u32[]{:S(2)}, u32[]{:S(2)}) collective-permute-start(bf16[4,2,16384]{2,1,0:T(2,128)(2,1)S(1)} %get-tuple-element.31), channel_id=1, source_target_pairs={{0,32},{16,48},{32,0},{48,16},{64,96},{80,112},{96,64},{112,80},{1... | collective-permute-start | bytes 786440 | tf_op jit(solution)/shard_map/ppermute | solution.py:180
  108.7 5.8 %collective-permute-start.13 = (bf16[2,2,16384]{2,1,0:T(2,128)(2,1)S(1)}, bf16[2,2,16384]{2,1,0:T(2,128)(2,1)S(1)}, u32[]{:S(2)}, u32[]{:S(2)}) collective-permute-start(bf16[2,2,16384]{2,1,0:T(2,128)(2,1)S(1)} %get-tuple-element.35), channel_id=1, source_target_pairs={{0,64},{16,80},{32,96},{48,112},{64,128},{80,144},{96,160},{112,17... | collective-permute-start | bytes 393224 | tf_op jit(solution)/shard_map/ppermute | solution.py:181
  110.3 4.2 %collective-permute-start.15 = (bf16[2,2,16384]{2,1,0:T(2,128)(2,1)S(1)}, bf16[2,2,16384]{2,1,0:T(2,128)(2,1)S(1)}, u32[]{:S(2)}, u32[]{:S(2)}) collective-permute-start(bf16[2,2,16384]{2,1,0:T(2,128)(2,1)S(1)} %get-tuple-element.36), channel_id=1, source_target_pairs={{0,192},{16,208},{32,224},{48,240},{64,0},{80,16},{96,32},{112,48}... | collective-permute-start | bytes 393224 | tf_op jit(solution)/shard_map/ppermute | solution.py:181
  111.8 7.0 %collective-permute-start.14 = (bf16[2,2,16384]{2,1,0:T(2,128)(2,1)S(1)}, bf16[2,2,16384]{2,1,0:T(2,128)(2,1)S(1)}, u32[]{:S(2)}, u32[]{:S(2)}) collective-permute-start(bf16[2,2,16384]{2,1,0:T(2,128)(2,1)S(1)} %get-tuple-element.37), channel_id=1, source_target_pairs={{0,128},{16,144},{32,160},{48,176},{64,192},{80,208},{96,224},{112... | collective-permute-start | bytes 393224 | tf_op jit(solution)/shard_map/ppermute | solution.py:181
  124.8 6.9 %copy-start.3 = (bf16[64,1,16,64]{0,3,2,1:T(8,128)(2,1)S(1)}, bf16[64,1,16,64]{0,3,2,1:T(8,128)(2,1)}, u32[]{:S(2)}) copy-start(bf16[64,1,16,64]{0,3,2,1:T(8,128)(2,1)} %copy-done.2) | copy-start | bytes 393220
  129.3 9.0 %copy-start.5 = (bf16[64,4096]{1,0:T(8,128)(2,1)S(1)}, bf16[64,4096]{1,0:T(8,128)(2,1)}, u32[]{:S(2)}) copy-start(bf16[64,4096]{1,0:T(8,128)(2,1)} %reduce-scatter.3.cloned.1.call-done) | copy-start | bytes 1572868
  130.4 8.0 %collective-permute-start.1 = (bf16[64,2048]{1,0:T(8,128)(2,1)S(1)}, bf16[64,2048]{1,0:T(8,128)(2,1)S(1)}, u32[]{:S(2)}, u32[]{:S(2)}) collective-permute-start(bf16[64,2048]{1,0:T(8,128)(2,1)S(1)} %slice.73), channel_id=1, source_target_pairs={{0,8},{1,9},{2,10},{3,11},{4,12},{5,13},{6,14},{7,15},{8,0},{9,1},... | collective-permute-start | bytes 786440 | tf_op jit(solution)/shard_map/ppermute | solution.py:248
Sparse Core Ops, SparseCore 0:
  28.9 57.6 reduce-scatter.2
  89.2 73.7 reduce-scatter.4

commit v2 on v1

--- a/solution.py
+++ b/solution.py
@@ -144,6 +144,39 @@
             flops=4 * rows * depth * size, bytes_accessed=3 * depth * size * 2, transcendentals=0
         ),
     )(kept, theirs, out_weight)
+
+
+def put_columns(array, piece, at):
+    rows, size = piece.shape
+    parts = [pl.ds(first, TILE) for first in range(0, size, TILE)]
+
+    def kernel(_, piece_ref, o_ref, held, came, gone):
+        reads = [pltpu.make_async_copy(piece_ref.at[:, p], held.at[:, p], came.at[i]) for i, p in enumerate(parts)]
+        writes = [
+            pltpu.make_async_copy(held.at[:, p], o_ref.at[:, pl.ds(at + i * TILE, TILE)], gone.at[i])
+            for i, p in enumerate(parts)
+        ]
+        for read in reads:
+            read.start()
+        for read, write in zip(reads, writes):
+            read.wait()
+            write.start()
+        for write in writes:
+            write.wait()
+
+    return pl.pallas_call(
+        kernel,
+        in_specs=[pl.BlockSpec(memory_space=pl.ANY)] * 2,
+        out_specs=pl.BlockSpec(memory_space=pl.ANY),
+        out_shape=jax.ShapeDtypeStruct(array.shape, array.dtype),
+        scratch_shapes=[
+            pltpu.VMEM((rows, size), BF),
+            pltpu.SemaphoreType.DMA((len(parts),)),
+            pltpu.SemaphoreType.DMA((len(parts),)),
+        ],
+        input_output_aliases={0: 0},
+        compiler_params=pltpu.CompilerParams(vmem_limit_bytes=VMEM),
+    )(array, piece)
 
 
 def sum_over_z(part):
@@ -247,9 +280,8 @@
     rest = sum_over_z(part)
     swapped = lax.ppermute(firsts[:, FIRST:], "head", X_SWAP)
     begin = (firsts[:, :FIRST].astype(F32) + swapped.astype(F32)).astype(BF)
-    attended = jnp.zeros((count // NZ, out_weight.shape[1]), BF)
-    for lo, piece in ((0, begin), (FIRST, rest)):
-        attended = lax.dynamic_update_slice(attended, piece, (0, lo))
+    begin = jnp.pad(begin, ((0, 0), (0, out_weight.shape[1] - FIRST)))
+    attended = put_columns(begin, rest, FIRST)
     victim_blocks, targets, free_order, _ = lax.optimization_barrier(
         (victim_blocks, destinations[:, 0], free_slots[0], part)
     )

time: 173 us -> 172 us (level)
  other arithmetic: 14.5 us -> 12.3 us
  Pallas kernels: 31.1 us -> 33.1 us
    dynamic_update_slice x1 -> x0, other arithmetic: 2.17 us -> none  [on_device(): attended = lax.dynamic_update_slice(attended, piece, (0, lo))]
    pallas_call x0 -> x1, Pallas kernels: none -> 1.96 us  [put_columns(): pl.pallas_call(kernel, in_specs=[pl.BlockSpec(memory_space=pl.ANY)] * 2,...]
  transfers between devices with their start and end apart: 18 -> 18, of which waited for: 11 -> 11; matrix products, arithmetic and copies ran while one was open for 16% -> 17% of each run, Pallas kernels for 14% -> 14%
where the time goes in v2:
time: 172 us
  waiting for transfers between devices  66.9 us (39%)
  Pallas kernels  33.1 us (19%)
  starting transfers between devices  23.5 us (14%)
  between operations  18.4 us (11%)
  local copies, waits for them, and re-layouts  14.1 us (8%)
  other arithmetic  12.3 us (7%)
  matrix products  3.53 us (2%)
    reduce_scatter x2, waiting for transfers between devices, sum_over_z(): lax.psum_scatter(part, 'head', scatter_dimension=0, axis_index_groups=Z_G...  23.5 us
    pallas_call x2, Pallas kernels, project(): pl.pallas_call(project_kernel, grid=((last - first) // TILE,), in_specs=[...  15.1 us
    ppermute x1, waiting for transfers between devices, on_device(): got.append(lax.ppermute(after(both, got[0]), 'head', X_SWAP))  12.2 us
    pallas_call x2, Pallas kernels, attend_half(): pl.pallas_call(functools.partial(attend_kernel, side), grid_spec=pltpu.Pr...  9.6 us
    ppermute x1, waiting for transfers between devices, migrate(): b = jnp.stack([b[:, 0], lax.ppermute(b[:, 1], 'dp', LO_SWAP)], axis=1)  7.58 us
    ppermute x4, waiting for transfers between devices, on_device(): near, far = (lax.ppermute(piece, 'dp', y_shift(k)) for k in (1, -1))  7.06 us
    pallas_call x1, Pallas kernels, project_first(): pl.pallas_call(project_first_kernel, grid=(2, tiles), in_specs=[pl.BlockS...  6.39 us
    ppermute x1, waiting for transfers between devices, on_device(): swapped = lax.ppermute(firsts[:, FIRST:], 'head', X_SWAP)  5.51 us
  transfers between devices with their start and end apart: 18, of which 11 were waited for; matrix products, arithmetic and copies ran while one was open for 17% of the time, Pallas kernels for 14%

profile of v2, /device:TPU:1, one launch (start us, length us, event | category | flops | bytes accessed | tf_op | source)
XLA Modules:
  0.0 171.8 jit_solution(9281794958412309296)
XLA Ops:
  7.3 1.2 fusion.49
  8.5 3.7 %collective-permute-start = (bf16[64,3072]{1,0:T(8,128)(2,1)S(1)}, bf16[64,3072]{1,0:T(8,128)(2,1)S(1)}, u32[]{:S(2)}, u32[]{:S(2)}) collective-permute-start(bf16[64,3072]{1,0:T(8,128)(2,1)S(1)} %get-tuple-element.29), channel_id=1, source_target_pairs={{0,8},{1,9},{2,10},{3,11},{4,12},{5,13},{6,14},{7,15},{8,0},{9,1},... | collective-permute-start | bytes 1179656 | tf_op jit(solution)/shard_map/ppermute | solution.py:258
  12.8 5.4 %shard_map.104.theirs_ref = bf16[512,512]{1,0:T(8,128)(2,1)} custom-call(s32[3]{0:T(128)} %pad_add_fusion.info, s32[1,4]{1,0:T(1,128)} %lengths.2, bf16[1024,512]{1,0:T(8,128)(2,1)} %q_ref.3, bf16[1024,1024]{1,0:T(8,128)(2,1)} %k_ref.3, bf16[1024,1024]{1,0:T(8,128)(2,1)} %v_ref.3), custom_call_target="tpu_custom_call" | custom-call | flops 805306368 | bytes 2097152 | tf_op jit(solution)/shard_map/pallas_call | solution.py:65
  18.1 4.2 %shard_map.105.kept_ref = bf16[512,512]{1,0:T(8,128)(2,1)} custom-call(s32[3]{0:T(128)} %pad_add_fusion.info, s32[1,4]{1,0:T(1,128)} %lengths.2, bf16[1024,512]{1,0:T(8,128)(2,1)} %q_ref.3, bf16[1024,1024]{1,0:T(8,128)(2,1)} %k_ref.3, bf16[1024,1024]{1,0:T(8,128)(2,1)} %v_ref.3), custom_call_target="tpu_custom_call" | custom-call | flops 805306368 | bytes 2097152 | tf_op jit(solution)/shard_map/pallas_call | solution.py:65
  22.4 6.4 %shard_map.106 = bf16[512,4096]{1,0:T(8,128)(2,1)} custom-call(bf16[512,512]{1,0:T(8,128)(2,1)} %shard_map.105.kept_ref, bf16[512,512]{1,0:T(8,128)(2,1)} %shard_map.104.theirs_ref, bf16[512,8192]{1,0:T(8,128)(2,1)} %w_ref.5), custom_call_target="tpu_custom_call" | custom-call | flops 2147483648 | bytes 6291456 | tf_op jit(solution)/shard_map/pallas_call | solution.py:132
  28.9 1.1 dynamic-slice.2
  30.0 1.3 collective-permute-start.3
  31.3 1.7 collective-permute-start.2
  33.1 2.9 %collective-permute-start.6 = (bf16[64,3072]{1,0:T(8,128)(2,1)S(1)}, bf16[64,3072]{1,0:T(8,128)(2,1)S(1)}, u32[]{:S(2)}, u32[]{:S(2)}) collective-permute-start(bf16[64,3072]{1,0:T(8,128)(2,1)S(1)} %collective-permute-done), channel_id=1, source_target_pairs={{0,128},{16,144},{32,160},{48,176},{64,192},{80,208},{96,224},{112... | collective-permute-start | bytes 1179656 | tf_op jit(solution)/shard_map/ppermute | solution.py:274
  36.0 0.8 collective-permute-start.5
  37.4 12.2 %collective-permute-done.3 = bf16[128,3072]{1,0:T(8,128)(2,1)S(1)} collective-permute-done((bf16[128,3072]{1,0:T(8,128)(2,1)S(1)}, bf16[128,3072]{1,0:T(8,128)(2,1)S(1)}, u32[]{:S(2)}, u32[]{:S(2)}) %collective-permute-start.3) | collective-permute-done | bytes 786464 | tf_op jit(solution)/shard_map/ppermute | solution.py:267
  49.7 3.6 %collective-permute-done.5 = bf16[64,3072]{1,0:T(8,128)(2,1)S(1)} collective-permute-done((bf16[64,3072]{1,0:T(8,128)(2,1)S(1)}, bf16[64,3072]{1,0:T(8,128)(2,1)S(1)}, u32[]{:S(2)}, u32[]{:S(2)}) %collective-permute-start.5) | collective-permute-done | bytes 393248 | tf_op jit(solution)/shard_map/ppermute | solution.py:272
  53.4 0.8 collective-permute-done.4
  54.1 1.3 collective-permute-start.8
  55.4 1.4 collective-permute-start.7
  57.0 3.9 %collective-permute-done.2 = bf16[512,512]{1,0:T(8,128)(2,1)S(1)} collective-permute-done((bf16[512,512]{1,0:T(8,128)(2,1)S(1)}, bf16[512,512]{1,0:T(8,128)(2,1)S(1)}, u32[]{:S(2)}, u32[]{:S(2)}) %collective-permute-start.2) | collective-permute-done | bytes 524320 | tf_op jit(solution)/shard_map/ppermute | solution.py:261
  60.9 1.9 %collective-permute-start.10 = (bf16[256,3072]{1,0:T(8,128)(2,1)S(1)}, bf16[256,3072]{1,0:T(8,128)(2,1)}, u32[]{:S(2)}, u32[]{:S(2)}) collective-permute-start(bf16[256,3072]{1,0:T(8,128)(2,1)S(1)} %pad_maximum_fusion.1.own_ref), channel_id=1, source_target_pairs={{0,16},{16,0},{32,48},{48,32},{64,80},{80,64},{96,112},{112,96},{1... | collective-permute-start | bytes 4718600 | tf_op jit(solution)/shard_map/ppermute | solution.py:277
  62.8 2.7 %collective-permute-done.8 = bf16[64,3072]{1,0:T(8,128)(2,1)S(1)} collective-permute-done((bf16[64,3072]{1,0:T(8,128)(2,1)S(1)}, bf16[64,3072]{1,0:T(8,128)(2,1)S(1)}, u32[]{:S(2)}, u32[]{:S(2)}) %collective-permute-start.8) | collective-permute-done | bytes 393248 | tf_op jit(solution)/shard_map/ppermute | solution.py:272
  65.5 1.3 pad_maximum_fusion.own_ref
  66.7 1.5 collective-permute-start.9
  68.3 1.3 convolution_convert_fusion.given_ref
  69.6 7.5 %shard_map.107.refs_0_ = bf16[512,6144]{1,0:T(8,128)(2,1)} custom-call(bf16[512,512]{1,0:T(8,128)(2,1)} %shard_map.105.kept_ref, bf16[512,512]{1,0:T(8,128)(2,1)} %convolution_convert_fusion.given_ref, bf16[512,8192]{1,0:T(8,128)(2,1)} %w_ref.5, bf16[256,3072]{1,0:T(8,128)(2,1)} %copy-done.1, bf16[256,3072]{1,0:T(8,128)(2,1)} %collective-permute-done.10.other_ref), custom_call_target="tpu_custom_call" | custom-call | flops 3221225472 | bytes 9437184 | tf_op jit(solution)/shard_map/pallas_call | solution.py:102
  77.2 7.6 %shard_map.108 = bf16[512,6144]{1,0:T(8,128)(2,1)} custom-call(bf16[512,512]{1,0:T(8,128)(2,1)} %shard_map.105.kept_ref, bf16[512,512]{1,0:T(8,128)(2,1)} %convolution_convert_fusion.given_ref, bf16[512,8192]{1,0:T(8,128)(2,1)} %w_ref.5, bf16[256,3072]{1,0:T(8,128)(2,1)} %pad_maximum_fusion.own_ref, ...), custom_call_target="tpu_custom_call", output_to_operand_aliasing={{}: (5, {})} | custom-call | flops 3221225472 | bytes 9437184 | tf_op jit(solution)/shard_map/pallas_call | solution.py:102
  89.3 1.4 constant_dynamic-slice_fusion.1
  93.1 1.6 copy.29
  94.7 0.7 reshape.190
  95.4 0.9 fusion.51
  96.9 1.5 collective-permute-done.11
  98.8 1.2 fusion.1
  100.4 7.6 %collective-permute-done.12 = bf16[4,2,16384]{2,1,0:T(2,128)(2,1)S(1)} collective-permute-done((bf16[4,2,16384]{2,1,0:T(2,128)(2,1)S(1)}, bf16[4,2,16384]{2,1,0:T(2,128)(2,1)S(1)}, u32[]{:S(2)}, u32[]{:S(2)}) %collective-permute-start.12) | collective-permute-done | bytes 262176 | tf_op jit(solution)/shard_map/ppermute | solution.py:213
  108.0 0.8 fusion.4
  108.7 1.6 collective-permute-start.13
  110.3 1.5 collective-permute-start.15
  111.8 1.3 collective-permute-start.14
  113.3 1.3 collective-permute-done.13
  114.6 4.2 %collective-permute-done.14 = bf16[2,2,16384]{2,1,0:T(2,128)(2,1)S(1)} collective-permute-done((bf16[2,2,16384]{2,1,0:T(2,128)(2,1)S(1)}, bf16[2,2,16384]{2,1,0:T(2,128)(2,1)S(1)}, u32[]{:S(2)}, u32[]{:S(2)}) %collective-permute-start.14) | collective-permute-done | bytes 131104 | tf_op jit(solution)/shard_map/ppermute | solution.py:214
  118.8 1.0 pad_maximum_fusion.4
  120.4 2.4 %compare_reduce_fusion = pred[128]{0:T(512)(128)(4,1)S(1)} fusion(bf16[128,2,16,64]{3,2,1,0:T(8,128)(2,1)S(1)} %reshape.191), kind=kLoop, calls=%fused_computation.25 | loop fusion | flops 256 | bytes 384 | tf_op jit(solution)/shard_map/lt | solution.py:216
  123.0 1.9 %copy.31 = bf16[128,2,16,64]{0,3,2,1:T(8,128)(2,1)} copy(bf16[128,2,16,64]{3,2,1,0:T(8,128)(2,1)S(1)} %broadcast_select_fusion) | data formatting | bytes 1048576 | tf_op jit(solution)/shard_map/jit(_where)/select_n | solution.py:228
  124.8 2.4 %fusion.9 = s32[128]{0:T(128)S(1)} fusion(bf16[128,2,16,64]{3,2,1,0:T(8,128)(2,1)S(1)} %reshape.191), kind=kLoop, calls=%fused_computation.34 | loop fusion | flops 384 | bytes 768 | tf_op jit(solution)/shard_map/convert_element_type | solution.py:218
  127.9 1.4 fusion.10
  129.4 1.0 slice.73
  130.4 1.3 collective-permute-start.1
  131.7 1.1 maximum_select_fusion
  132.9 5.5 %collective-permute-done.1 = bf16[64,2048]{1,0:T(8,128)(2,1)S(1)} collective-permute-done((bf16[64,2048]{1,0:T(8,128)(2,1)S(1)}, bf16[64,2048]{1,0:T(8,128)(2,1)S(1)}, u32[]{:S(2)}, u32[]{:S(2)}) %collective-permute-start.1) | collective-permute-done | bytes 262176 | tf_op jit(solution)/shard_map/ppermute | solution.py:281
  138.4 1.0 pad.4._
  139.5 23.5 %reduce-scatter.5.cloned.1.call-done.piece_ref = bf16[64,6144]{1,0:T(8,128)(2,1)} async-done(((bf16[512,6144]{1,0:T(8,128)(2,1)}), bf16[64,6144]{1,0:T(8,128)(2,1)}) %reduce-scatter.5.cloned.1.call-update) | async-done | bytes 786448 | tf_op jit(solution)/shard_map/reduce_scatter | solution.py:183
  162.9 2.0 %shard_map.109 = bf16[64,8192]{1,0:T(8,128)(2,1)} custom-call(bf16[64,8192]{1,0:T(8,128)(2,1)} %pad.4._, bf16[64,6144]{1,0:T(8,128)(2,1)} %reduce-scatter.5.cloned.1.call-done.piece_ref), custom_call_target="tpu_custom_call", output_to_operand_aliasing={{}: (0, {})} | custom-call | tf_op jit(solution)/shard_map/pallas_call | solution.py:167
  (64 shorter events, 7.6 us)
Async XLA Ops:
  7.2 85.2 %copy-start = (bf16[128,2,16,64]{0,3,2,1:T(8,128)(2,1)S(1)}, bf16[128,2,16,64]{0,3,2,1:T(8,128)(2,1)}, u32[]{:S(2)}) copy-start(bf16[128,2,16,64]{0,3,2,1:T(8,128)(2,1)} %param.14) | copy-start | bytes 1572868
  7.2 122.2 %reduce-scatter.3.cloned.1.call-start = ((), (), s32[]{:S(2)}) async-start(), calls=%async_computation.2 | async-start | bytes 4718592 | tf_op jit(solution)/shard_map/reduce_scatter | solution.py:183
  8.5 13.9 %collective-permute-start = (bf16[64,3072]{1,0:T(8,128)(2,1)S(1)}, bf16[64,3072]{1,0:T(8,128)(2,1)S(1)}, u32[]{:S(2)}, u32[]{:S(2)}) collective-permute-start(bf16[64,3072]{1,0:T(8,128)(2,1)S(1)} %get-tuple-element.29), channel_id=1, source_target_pairs={{0,8},{1,9},{2,10},{3,11},{4,12},{5,13},{6,14},{7,15},{8,0},{9,1},... | collective-permute-start | bytes 1179656 | tf_op jit(solution)/shard_map/ppermute | solution.py:258
  28.8 2.6 %copy-start.4 = (bf16[512,512]{1,0:T(8,128)(2,1)S(1)}, bf16[512,512]{1,0:T(8,128)(2,1)}, u32[]{:S(2)}) copy-start(bf16[512,512]{1,0:T(8,128)(2,1)} %shard_map.104.theirs_ref) | copy-start | bytes 1572868
  28.8 134.2 %reduce-scatter.5.cloned.1.call-start = ((), (), s32[]{:S(2)}) async-start(), calls=%async_computation.3 | async-start | bytes 7077888 | tf_op jit(solution)/shard_map/reduce_scatter | solution.py:183
  30.0 19.7 %collective-permute-start.3 = (bf16[128,3072]{1,0:T(8,128)(2,1)S(1)}, bf16[128,3072]{1,0:T(8,128)(2,1)S(1)}, u32[]{:S(2)}, u32[]{:S(2)}) collective-permute-start(bf16[128,3072]{1,0:T(8,128)(2,1)S(1)} %pad_maximum_fusion.2), channel_id=1, source_target_pairs={{0,8},{1,9},{2,10},{3,11},{4,12},{5,13},{6,14},{7,15},{8,0},{9,1},... | collective-permute-start | bytes 2359304 | tf_op jit(solution)/shard_map/ppermute | solution.py:267
  31.3 29.6 %collective-permute-start.2 = (bf16[512,512]{1,0:T(8,128)(2,1)S(1)}, bf16[512,512]{1,0:T(8,128)(2,1)S(1)}, u32[]{:S(2)}, u32[]{:S(2)}) collective-permute-start(bf16[512,512]{1,0:T(8,128)(2,1)S(1)} %copy-done.4), channel_id=1, source_target_pairs={{0,8},{1,9},{2,10},{3,11},{4,12},{5,13},{6,14},{7,15},{8,0},{9,1},... | collective-permute-start | bytes 1572872 | tf_op jit(solution)/shard_map/ppermute | solution.py:261
  33.1 16.7 %collective-permute-start.6 = (bf16[64,3072]{1,0:T(8,128)(2,1)S(1)}, bf16[64,3072]{1,0:T(8,128)(2,1)S(1)}, u32[]{:S(2)}, u32[]{:S(2)}) collective-permute-start(bf16[64,3072]{1,0:T(8,128)(2,1)S(1)} %collective-permute-done), channel_id=1, source_target_pairs={{0,128},{16,144},{32,160},{48,176},{64,192},{80,208},{96,224},{112... | collective-permute-start | bytes 1179656 | tf_op jit(solution)/shard_map/ppermute | solution.py:274
  36.0 17.4 %collective-permute-start.5 = (bf16[64,3072]{1,0:T(8,128)(2,1)S(1)}, bf16[64,3072]{1,0:T(8,128)(2,1)S(1)}, u32[]{:S(2)}, u32[]{:S(2)}) collective-permute-start(bf16[64,3072]{1,0:T(8,128)(2,1)S(1)} %collective-permute-done), channel_id=1, source_target_pairs={{0,192},{16,208},{32,224},{48,240},{64,0},{80,16},{96,32},{112,48}... | collective-permute-start | bytes 1179656 | tf_op jit(solution)/shard_map/ppermute | solution.py:272
  36.8 17.4 %collective-permute-start.4 = (bf16[64,3072]{1,0:T(8,128)(2,1)S(1)}, bf16[64,3072]{1,0:T(8,128)(2,1)S(1)}, u32[]{:S(2)}, u32[]{:S(2)}) collective-permute-start(bf16[64,3072]{1,0:T(8,128)(2,1)S(1)} %collective-permute-done), channel_id=1, source_target_pairs={{0,64},{16,80},{32,96},{48,112},{64,128},{80,144},{96,160},{112,17... | collective-permute-start | bytes 1179656 | tf_op jit(solution)/shard_map/ppermute | solution.py:272
  54.1 11.3 %collective-permute-start.8 = (bf16[64,3072]{1,0:T(8,128)(2,1)S(1)}, bf16[64,3072]{1,0:T(8,128)(2,1)S(1)}, u32[]{:S(2)}, u32[]{:S(2)}) collective-permute-start(bf16[64,3072]{1,0:T(8,128)(2,1)S(1)} %get-tuple-element.20), channel_id=1, source_target_pairs={{0,64},{16,80},{32,96},{48,112},{64,128},{80,144},{96,160},{112,17... | collective-permute-start | bytes 1179656 | tf_op jit(solution)/shard_map/ppermute | solution.py:272
  55.4 10.0 %collective-permute-start.7 = (bf16[64,3072]{1,0:T(8,128)(2,1)S(1)}, bf16[64,3072]{1,0:T(8,128)(2,1)S(1)}, u32[]{:S(2)}, u32[]{:S(2)}) collective-permute-start(bf16[64,3072]{1,0:T(8,128)(2,1)S(1)} %get-tuple-element.20), channel_id=1, source_target_pairs={{0,192},{16,208},{32,224},{48,240},{64,0},{80,16},{96,32},{112,48}... | collective-permute-start | bytes 1179656 | tf_op jit(solution)/shard_map/ppermute | solution.py:272
  57.0 12.6 %copy-start.1 = (bf16[256,3072]{1,0:T(8,128)(2,1)}, bf16[256,3072]{1,0:T(8,128)(2,1)S(1)}, u32[]{:S(2)}) copy-start(bf16[256,3072]{1,0:T(8,128)(2,1)S(1)} %pad_maximum_fusion.1.own_ref) | copy-start | bytes 4718596
  60.9 8.7 %collective-permute-start.10 = (bf16[256,3072]{1,0:T(8,128)(2,1)S(1)}, bf16[256,3072]{1,0:T(8,128)(2,1)}, u32[]{:S(2)}, u32[]{:S(2)}) collective-permute-start(bf16[256,3072]{1,0:T(8,128)(2,1)S(1)} %pad_maximum_fusion.1.own_ref), channel_id=1, source_target_pairs={{0,16},{16,0},{32,48},{48,32},{64,80},{80,64},{96,112},{112,96},{1... | collective-permute-start | bytes 4718600 | tf_op jit(solution)/shard_map/ppermute | solution.py:277
  66.7 10.4 %collective-permute-start.9 = (bf16[256,3072]{1,0:T(8,128)(2,1)}, bf16[256,3072]{1,0:T(8,128)(2,1)}, u32[]{:S(2)}, u32[]{:S(2)}) collective-permute-start(bf16[256,3072]{1,0:T(8,128)(2,1)} %pad_maximum_fusion.own_ref), channel_id=1, source_target_pairs={{0,16},{16,0},{32,48},{48,32},{64,80},{80,64},{96,112},{112,96},{1... | collective-permute-start | bytes 4718600 | tf_op jit(solution)/shard_map/ppermute | solution.py:277
  77.2 7.6 %copy-start.6 = (s32[64,1]{0,1:T(1,128)S(1)}, s32[64,1]{0,1:T(1,128)}, u32[]{:S(2)}) copy-start(s32[64,1]{0,1:T(1,128)} %param.16) | copy-start | bytes 772
  84.9 3.4 %copy-start.7 = (s32[64]{0:T(128)S(1)}, s32[64]{0:T(128)}, u32[]{:S(2)}) copy-start(s32[64]{0:T(128)} %param.15) | copy-start | bytes 772
  91.3 1.6 copy-start.2
  96.3 16.8 %copy-start.8 = (s32[1,128]{1,0:T(1,128)S(1)}, s32[1,128]{1,0:T(1,128)}, u32[]{:S(2)}) copy-start(s32[1,128]{1,0:T(1,128)} %param.17) | copy-start | bytes 1540
  96.8 1.6 collective-permute-start.11
  100.0 8.0 %collective-permute-start.12 = (bf16[4,2,16384]{2,1,0:T(2,128)(2,1)S(1)}, bf16[4,2,16384]{2,1,0:T(2,128)(2,1)S(1)}, u32[]{:S(2)}, u32[]{:S(2)}) collective-permute-start(bf16[4,2,16384]{2,1,0:T(2,128)(2,1)S(1)} %get-tuple-element.31), channel_id=1, source_target_pairs={{0,32},{16,48},{32,0},{48,16},{64,96},{80,112},{96,64},{112,80},{1... | collective-permute-start | bytes 786440 | tf_op jit(solution)/shard_map/ppermute | solution.py:213
  108.7 5.8 %collective-permute-start.13 = (bf16[2,2,16384]{2,1,0:T(2,128)(2,1)S(1)}, bf16[2,2,16384]{2,1,0:T(2,128)(2,1)S(1)}, u32[]{:S(2)}, u32[]{:S(2)}) collective-permute-start(bf16[2,2,16384]{2,1,0:T(2,128)(2,1)S(1)} %get-tuple-element.35), channel_id=1, source_target_pairs={{0,64},{16,80},{32,96},{48,112},{64,128},{80,144},{96,160},{112,17... | collective-permute-start | bytes 393224 | tf_op jit(solution)/shard_map/ppermute | solution.py:214
  110.3 4.2 %collective-permute-start.15 = (bf16[2,2,16384]{2,1,0:T(2,128)(2,1)S(1)}, bf16[2,2,16384]{2,1,0:T(2,128)(2,1)S(1)}, u32[]{:S(2)}, u32[]{:S(2)}) collective-permute-start(bf16[2,2,16384]{2,1,0:T(2,128)(2,1)S(1)} %get-tuple-element.36), channel_id=1, source_target_pairs={{0,192},{16,208},{32,224},{48,240},{64,0},{80,16},{96,32},{112,48}... | collective-permute-start | bytes 393224 | tf_op jit(solution)/shard_map/ppermute | solution.py:214
  111.8 7.0 %collective-permute-start.14 = (bf16[2,2,16384]{2,1,0:T(2,128)(2,1)S(1)}, bf16[2,2,16384]{2,1,0:T(2,128)(2,1)S(1)}, u32[]{:S(2)}, u32[]{:S(2)}) collective-permute-start(bf16[2,2,16384]{2,1,0:T(2,128)(2,1)S(1)} %get-tuple-element.37), channel_id=1, source_target_pairs={{0,128},{16,144},{32,160},{48,176},{64,192},{80,208},{96,224},{112... | collective-permute-start | bytes 393224 | tf_op jit(solution)/shard_map/ppermute | solution.py:214
  124.8 6.9 %copy-start.3 = (bf16[64,1,16,64]{0,3,2,1:T(8,128)(2,1)S(1)}, bf16[64,1,16,64]{0,3,2,1:T(8,128)(2,1)}, u32[]{:S(2)}) copy-start(bf16[64,1,16,64]{0,3,2,1:T(8,128)(2,1)} %copy-done.2) | copy-start | bytes 393220
  129.3 9.0 %copy-start.5 = (bf16[64,4096]{1,0:T(8,128)(2,1)S(1)}, bf16[64,4096]{1,0:T(8,128)(2,1)}, u32[]{:S(2)}) copy-start(bf16[64,4096]{1,0:T(8,128)(2,1)} %reduce-scatter.3.cloned.1.call-done) | copy-start | bytes 1572868
  130.4 8.0 %collective-permute-start.1 = (bf16[64,2048]{1,0:T(8,128)(2,1)S(1)}, bf16[64,2048]{1,0:T(8,128)(2,1)S(1)}, u32[]{:S(2)}, u32[]{:S(2)}) collective-permute-start(bf16[64,2048]{1,0:T(8,128)(2,1)S(1)} %slice.73), channel_id=1, source_target_pairs={{0,8},{1,9},{2,10},{3,11},{4,12},{5,13},{6,14},{7,15},{8,0},{9,1},... | collective-permute-start | bytes 786440 | tf_op jit(solution)/shard_map/ppermute | solution.py:281
Sparse Core Ops, SparseCore 0:
  28.9 57.6 reduce-scatter.2
  89.2 73.7 reduce-scatter.4

commit v3 on v2

--- a/solution.py
+++ b/solution.py
@@ -148,12 +148,13 @@
 
 def put_columns(array, piece, at):
     rows, size = piece.shape
-    parts = [pl.ds(first, TILE) for first in range(0, size, TILE)]
+    width = 2 * TILE
+    parts = [pl.ds(first, width) for first in range(0, size, width)]
 
     def kernel(_, piece_ref, o_ref, held, came, gone):
         reads = [pltpu.make_async_copy(piece_ref.at[:, p], held.at[:, p], came.at[i]) for i, p in enumerate(parts)]
         writes = [
-            pltpu.make_async_copy(held.at[:, p], o_ref.at[:, pl.ds(at + i * TILE, TILE)], gone.at[i])
+            pltpu.make_async_copy(held.at[:, p], o_ref.at[:, pl.ds(at + i * width, width)], gone.at[i])
             for i, p in enumerate(parts)
         ]
         for read in reads:

time: 172 us -> 172 us (level)
  no operation moved by 1% of the time
where the time goes in v3:
time: 172 us
  waiting for transfers between devices  66.9 us (39%)
  Pallas kernels  33 us (19%)
  starting transfers between devices  23.5 us (14%)
  between operations  18.4 us (11%)
  local copies, waits for them, and re-layouts  14.1 us (8%)
  other arithmetic  12.3 us (7%)
  matrix products  3.53 us (2%)
    reduce_scatter x2, waiting for transfers between devices, sum_over_z(): lax.psum_scatter(part, 'head', scatter_dimension=0, axis_index_groups=Z_G...  23.5 us
    pallas_call x2, Pallas kernels, project(): pl.pallas_call(project_kernel, grid=((last - first) // TILE,), in_specs=[...  15.1 us
    ppermute x1, waiting for transfers between devices, on_device(): got.append(lax.ppermute(after(both, got[0]), 'head', X_SWAP))  12.2 us
    pallas_call x2, Pallas kernels, attend_half(): pl.pallas_call(functools.partial(attend_kernel, side), grid_spec=pltpu.Pr...  9.6 us
    ppermute x1, waiting for transfers between devices, migrate(): b = jnp.stack([b[:, 0], lax.ppermute(b[:, 1], 'dp', LO_SWAP)], axis=1)  7.58 us
    ppermute x4, waiting for transfers between devices, on_device(): near, far = (lax.ppermute(piece, 'dp', y_shift(k)) for k in (1, -1))  7.06 us
    pallas_call x1, Pallas kernels, project_first(): pl.pallas_call(project_first_kernel, grid=(2, tiles), in_specs=[pl.BlockS...  6.39 us
    ppermute x1, waiting for transfers between devices, on_device(): swapped = lax.ppermute(firsts[:, FIRST:], 'head', X_SWAP)  5.51 us
  transfers between devices with their start and end apart: 18, of which 11 were waited for; matrix products, arithmetic and copies ran while one was open for 17% of the time, Pallas kernels for 14%

profile of v3, /device:TPU:1, one launch (start us, length us, event | category | flops | bytes accessed | tf_op | source)
XLA Modules:
  0.0 171.7 jit_solution(11516291902523231559)
XLA Ops:
  7.3 1.2 fusion.49
  8.5 3.7 %collective-permute-start = (bf16[64,3072]{1,0:T(8,128)(2,1)S(1)}, bf16[64,3072]{1,0:T(8,128)(2,1)S(1)}, u32[]{:S(2)}, u32[]{:S(2)}) collective-permute-start(bf16[64,3072]{1,0:T(8,128)(2,1)S(1)} %get-tuple-element.29), channel_id=1, source_target_pairs={{0,8},{1,9},{2,10},{3,11},{4,12},{5,13},{6,14},{7,15},{8,0},{9,1},... | collective-permute-start | bytes 1179656 | tf_op jit(solution)/shard_map/ppermute | solution.py:259
  12.8 5.4 %shard_map.104.theirs_ref = bf16[512,512]{1,0:T(8,128)(2,1)} custom-call(s32[3]{0:T(128)} %pad_add_fusion.info, s32[1,4]{1,0:T(1,128)} %lengths.2, bf16[1024,512]{1,0:T(8,128)(2,1)} %q_ref.3, bf16[1024,1024]{1,0:T(8,128)(2,1)} %k_ref.3, bf16[1024,1024]{1,0:T(8,128)(2,1)} %v_ref.3), custom_call_target="tpu_custom_call" | custom-call | flops 805306368 | bytes 2097152 | tf_op jit(solution)/shard_map/pallas_call | solution.py:65
  18.1 4.2 %shard_map.105.kept_ref = bf16[512,512]{1,0:T(8,128)(2,1)} custom-call(s32[3]{0:T(128)} %pad_add_fusion.info, s32[1,4]{1,0:T(1,128)} %lengths.2, bf16[1024,512]{1,0:T(8,128)(2,1)} %q_ref.3, bf16[1024,1024]{1,0:T(8,128)(2,1)} %k_ref.3, bf16[1024,1024]{1,0:T(8,128)(2,1)} %v_ref.3), custom_call_target="tpu_custom_call" | custom-call | flops 805306368 | bytes 2097152 | tf_op jit(solution)/shard_map/pallas_call | solution.py:65
  22.4 6.4 %shard_map.106 = bf16[512,4096]{1,0:T(8,128)(2,1)} custom-call(bf16[512,512]{1,0:T(8,128)(2,1)} %shard_map.105.kept_ref, bf16[512,512]{1,0:T(8,128)(2,1)} %shard_map.104.theirs_ref, bf16[512,8192]{1,0:T(8,128)(2,1)} %w_ref.5), custom_call_target="tpu_custom_call" | custom-call | flops 2147483648 | bytes 6291456 | tf_op jit(solution)/shard_map/pallas_call | solution.py:132
  28.9 1.1 dynamic-slice.2
  30.0 1.3 collective-permute-start.3
  31.3 1.7 collective-permute-start.2
  33.1 2.9 %collective-permute-start.6 = (bf16[64,3072]{1,0:T(8,128)(2,1)S(1)}, bf16[64,3072]{1,0:T(8,128)(2,1)S(1)}, u32[]{:S(2)}, u32[]{:S(2)}) collective-permute-start(bf16[64,3072]{1,0:T(8,128)(2,1)S(1)} %collective-permute-done), channel_id=1, source_target_pairs={{0,128},{16,144},{32,160},{48,176},{64,192},{80,208},{96,224},{112... | collective-permute-start | bytes 1179656 | tf_op jit(solution)/shard_map/ppermute | solution.py:275
  36.0 0.8 collective-permute-start.5
  37.4 12.2 %collective-permute-done.3 = bf16[128,3072]{1,0:T(8,128)(2,1)S(1)} collective-permute-done((bf16[128,3072]{1,0:T(8,128)(2,1)S(1)}, bf16[128,3072]{1,0:T(8,128)(2,1)S(1)}, u32[]{:S(2)}, u32[]{:S(2)}) %collective-permute-start.3) | collective-permute-done | bytes 786464 | tf_op jit(solution)/shard_map/ppermute | solution.py:268
  49.7 3.6 %collective-permute-done.5 = bf16[64,3072]{1,0:T(8,128)(2,1)S(1)} collective-permute-done((bf16[64,3072]{1,0:T(8,128)(2,1)S(1)}, bf16[64,3072]{1,0:T(8,128)(2,1)S(1)}, u32[]{:S(2)}, u32[]{:S(2)}) %collective-permute-start.5) | collective-permute-done | bytes 393248 | tf_op jit(solution)/shard_map/ppermute | solution.py:273
  53.4 0.8 collective-permute-done.4
  54.1 1.3 collective-permute-start.8
  55.4 1.4 collective-permute-start.7
  57.0 3.9 %collective-permute-done.2 = bf16[512,512]{1,0:T(8,128)(2,1)S(1)} collective-permute-done((bf16[512,512]{1,0:T(8,128)(2,1)S(1)}, bf16[512,512]{1,0:T(8,128)(2,1)S(1)}, u32[]{:S(2)}, u32[]{:S(2)}) %collective-permute-start.2) | collective-permute-done | bytes 524320 | tf_op jit(solution)/shard_map/ppermute | solution.py:262
  60.9 1.9 %collective-permute-start.10 = (bf16[256,3072]{1,0:T(8,128)(2,1)S(1)}, bf16[256,3072]{1,0:T(8,128)(2,1)}, u32[]{:S(2)}, u32[]{:S(2)}) collective-permute-start(bf16[256,3072]{1,0:T(8,128)(2,1)S(1)} %pad_maximum_fusion.1.own_ref), channel_id=1, source_target_pairs={{0,16},{16,0},{32,48},{48,32},{64,80},{80,64},{96,112},{112,96},{1... | collective-permute-start | bytes 4718600 | tf_op jit(solution)/shard_map/ppermute | solution.py:278
  62.8 2.7 %collective-permute-done.8 = bf16[64,3072]{1,0:T(8,128)(2,1)S(1)} collective-permute-done((bf16[64,3072]{1,0:T(8,128)(2,1)S(1)}, bf16[64,3072]{1,0:T(8,128)(2,1)S(1)}, u32[]{:S(2)}, u32[]{:S(2)}) %collective-permute-start.8) | collective-permute-done | bytes 393248 | tf_op jit(solution)/shard_map/ppermute | solution.py:273
  65.5 1.3 pad_maximum_fusion.own_ref
  66.7 1.5 collective-permute-start.9
  68.3 1.3 convolution_convert_fusion.given_ref
  69.6 7.5 %shard_map.107.refs_0_ = bf16[512,6144]{1,0:T(8,128)(2,1)} custom-call(bf16[512,512]{1,0:T(8,128)(2,1)} %shard_map.105.kept_ref, bf16[512,512]{1,0:T(8,128)(2,1)} %convolution_convert_fusion.given_ref, bf16[512,8192]{1,0:T(8,128)(2,1)} %w_ref.5, bf16[256,3072]{1,0:T(8,128)(2,1)} %copy-done.1, bf16[256,3072]{1,0:T(8,128)(2,1)} %collective-permute-done.10.other_ref), custom_call_target="tpu_custom_call" | custom-call | flops 3221225472 | bytes 9437184 | tf_op jit(solution)/shard_map/pallas_call | solution.py:102
  77.2 7.6 %shard_map.108 = bf16[512,6144]{1,0:T(8,128)(2,1)} custom-call(bf16[512,512]{1,0:T(8,128)(2,1)} %shard_map.105.kept_ref, bf16[512,512]{1,0:T(8,128)(2,1)} %convolution_convert_fusion.given_ref, bf16[512,8192]{1,0:T(8,128)(2,1)} %w_ref.5, bf16[256,3072]{1,0:T(8,128)(2,1)} %pad_maximum_fusion.own_ref, ...), custom_call_target="tpu_custom_call", output_to_operand_aliasing={{}: (5, {})} | custom-call | flops 3221225472 | bytes 9437184 | tf_op jit(solution)/shard_map/pallas_call | solution.py:102
  89.3 1.4 constant_dynamic-slice_fusion.1
  93.1 1.6 copy.29
  94.7 0.7 reshape.190
  95.4 0.9 fusion.51
  96.9 1.5 collective-permute-done.11
  98.8 1.2 fusion.1
  100.4 7.6 %collective-permute-done.12 = bf16[4,2,16384]{2,1,0:T(2,128)(2,1)S(1)} collective-permute-done((bf16[4,2,16384]{2,1,0:T(2,128)(2,1)S(1)}, bf16[4,2,16384]{2,1,0:T(2,128)(2,1)S(1)}, u32[]{:S(2)}, u32[]{:S(2)}) %collective-permute-start.12) | collective-permute-done | bytes 262176 | tf_op jit(solution)/shard_map/ppermute | solution.py:214
  108.0 0.8 fusion.4
  108.7 1.6 collective-permute-start.13
  110.3 1.5 collective-permute-start.15
  111.8 1.3 collective-permute-start.14
  113.3 1.3 collective-permute-done.13
  114.6 4.2 %collective-permute-done.14 = bf16[2,2,16384]{2,1,0:T(2,128)(2,1)S(1)} collective-permute-done((bf16[2,2,16384]{2,1,0:T(2,128)(2,1)S(1)}, bf16[2,2,16384]{2,1,0:T(2,128)(2,1)S(1)}, u32[]{:S(2)}, u32[]{:S(2)}) %collective-permute-start.14) | collective-permute-done | bytes 131104 | tf_op jit(solution)/shard_map/ppermute | solution.py:215
  118.8 1.0 pad_maximum_fusion.4
  120.4 2.4 %compare_reduce_fusion = pred[128]{0:T(512)(128)(4,1)S(1)} fusion(bf16[128,2,16,64]{3,2,1,0:T(8,128)(2,1)S(1)} %reshape.191), kind=kLoop, calls=%fused_computation.25 | loop fusion | flops 256 | bytes 384 | tf_op jit(solution)/shard_map/lt | solution.py:217
  123.0 1.9 %copy.31 = bf16[128,2,16,64]{0,3,2,1:T(8,128)(2,1)} copy(bf16[128,2,16,64]{3,2,1,0:T(8,128)(2,1)S(1)} %broadcast_select_fusion) | data formatting | bytes 1048576 | tf_op jit(solution)/shard_map/jit(_where)/select_n | solution.py:229
  124.8 2.4 %fusion.9 = s32[128]{0:T(128)S(1)} fusion(bf16[128,2,16,64]{3,2,1,0:T(8,128)(2,1)S(1)} %reshape.191), kind=kLoop, calls=%fused_computation.34 | loop fusion | flops 384 | bytes 768 | tf_op jit(solution)/shard_map/convert_element_type | solution.py:219
  127.9 1.4 fusion.10
  129.4 1.0 slice.73
  130.4 1.3 collective-permute-start.1
  131.7 1.1 maximum_select_fusion
  132.9 5.5 %collective-permute-done.1 = bf16[64,2048]{1,0:T(8,128)(2,1)S(1)} collective-permute-done((bf16[64,2048]{1,0:T(8,128)(2,1)S(1)}, bf16[64,2048]{1,0:T(8,128)(2,1)S(1)}, u32[]{:S(2)}, u32[]{:S(2)}) %collective-permute-start.1) | collective-permute-done | bytes 262176 | tf_op jit(solution)/shard_map/ppermute | solution.py:282
  138.4 1.0 pad.4._
  139.5 23.5 %reduce-scatter.5.cloned.1.call-done.piece_ref = bf16[64,6144]{1,0:T(8,128)(2,1)} async-done(((bf16[512,6144]{1,0:T(8,128)(2,1)}), bf16[64,6144]{1,0:T(8,128)(2,1)}) %reduce-scatter.5.cloned.1.call-update) | async-done | bytes 786448 | tf_op jit(solution)/shard_map/reduce_scatter | solution.py:184
  162.9 1.9 %shard_map.109 = bf16[64,8192]{1,0:T(8,128)(2,1)} custom-call(bf16[64,8192]{1,0:T(8,128)(2,1)} %pad.4._, bf16[64,6144]{1,0:T(8,128)(2,1)} %reduce-scatter.5.cloned.1.call-done.piece_ref), custom_call_target="tpu_custom_call", output_to_operand_aliasing={{}: (0, {})} | custom-call | tf_op jit(solution)/shard_map/pallas_call | solution.py:168
  (64 shorter events, 7.6 us)
Async XLA Ops:
  7.2 85.2 %copy-start = (bf16[128,2,16,64]{0,3,2,1:T(8,128)(2,1)S(1)}, bf16[128,2,16,64]{0,3,2,1:T(8,128)(2,1)}, u32[]{:S(2)}) copy-start(bf16[128,2,16,64]{0,3,2,1:T(8,128)(2,1)} %param.14) | copy-start | bytes 1572868
  7.2 122.2 %reduce-scatter.3.cloned.1.call-start = ((), (), s32[]{:S(2)}) async-start(), calls=%async_computation.2 | async-start | bytes 4718592 | tf_op jit(solution)/shard_map/reduce_scatter | solution.py:184
  8.5 13.9 %collective-permute-start = (bf16[64,3072]{1,0:T(8,128)(2,1)S(1)}, bf16[64,3072]{1,0:T(8,128)(2,1)S(1)}, u32[]{:S(2)}, u32[]{:S(2)}) collective-permute-start(bf16[64,3072]{1,0:T(8,128)(2,1)S(1)} %get-tuple-element.29), channel_id=1, source_target_pairs={{0,8},{1,9},{2,10},{3,11},{4,12},{5,13},{6,14},{7,15},{8,0},{9,1},... | collective-permute-start | bytes 1179656 | tf_op jit(solution)/shard_map/ppermute | solution.py:259
  28.8 2.6 %copy-start.4 = (bf16[512,512]{1,0:T(8,128)(2,1)S(1)}, bf16[512,512]{1,0:T(8,128)(2,1)}, u32[]{:S(2)}) copy-start(bf16[512,512]{1,0:T(8,128)(2,1)} %shard_map.104.theirs_ref) | copy-start | bytes 1572868
  28.8 134.2 %reduce-scatter.5.cloned.1.call-start = ((), (), s32[]{:S(2)}) async-start(), calls=%async_computation.3 | async-start | bytes 7077888 | tf_op jit(solution)/shard_map/reduce_scatter | solution.py:184
  30.0 19.7 %collective-permute-start.3 = (bf16[128,3072]{1,0:T(8,128)(2,1)S(1)}, bf16[128,3072]{1,0:T(8,128)(2,1)S(1)}, u32[]{:S(2)}, u32[]{:S(2)}) collective-permute-start(bf16[128,3072]{1,0:T(8,128)(2,1)S(1)} %pad_maximum_fusion.2), channel_id=1, source_target_pairs={{0,8},{1,9},{2,10},{3,11},{4,12},{5,13},{6,14},{7,15},{8,0},{9,1},... | collective-permute-start | bytes 2359304 | tf_op jit(solution)/shard_map/ppermute | solution.py:268
  31.3 29.6 %collective-permute-start.2 = (bf16[512,512]{1,0:T(8,128)(2,1)S(1)}, bf16[512,512]{1,0:T(8,128)(2,1)S(1)}, u32[]{:S(2)}, u32[]{:S(2)}) collective-permute-start(bf16[512,512]{1,0:T(8,128)(2,1)S(1)} %copy-done.4), channel_id=1, source_target_pairs={{0,8},{1,9},{2,10},{3,11},{4,12},{5,13},{6,14},{7,15},{8,0},{9,1},... | collective-permute-start | bytes 1572872 | tf_op jit(solution)/shard_map/ppermute | solution.py:262
  33.1 16.7 %collective-permute-start.6 = (bf16[64,3072]{1,0:T(8,128)(2,1)S(1)}, bf16[64,3072]{1,0:T(8,128)(2,1)S(1)}, u32[]{:S(2)}, u32[]{:S(2)}) collective-permute-start(bf16[64,3072]{1,0:T(8,128)(2,1)S(1)} %collective-permute-done), channel_id=1, source_target_pairs={{0,128},{16,144},{32,160},{48,176},{64,192},{80,208},{96,224},{112... | collective-permute-start | bytes 1179656 | tf_op jit(solution)/shard_map/ppermute | solution.py:275
  36.0 17.4 %collective-permute-start.5 = (bf16[64,3072]{1,0:T(8,128)(2,1)S(1)}, bf16[64,3072]{1,0:T(8,128)(2,1)S(1)}, u32[]{:S(2)}, u32[]{:S(2)}) collective-permute-start(bf16[64,3072]{1,0:T(8,128)(2,1)S(1)} %collective-permute-done), channel_id=1, source_target_pairs={{0,192},{16,208},{32,224},{48,240},{64,0},{80,16},{96,32},{112,48}... | collective-permute-start | bytes 1179656 | tf_op jit(solution)/shard_map/ppermute | solution.py:273
  36.8 17.4 %collective-permute-start.4 = (bf16[64,3072]{1,0:T(8,128)(2,1)S(1)}, bf16[64,3072]{1,0:T(8,128)(2,1)S(1)}, u32[]{:S(2)}, u32[]{:S(2)}) collective-permute-start(bf16[64,3072]{1,0:T(8,128)(2,1)S(1)} %collective-permute-done), channel_id=1, source_target_pairs={{0,64},{16,80},{32,96},{48,112},{64,128},{80,144},{96,160},{112,17... | collective-permute-start | bytes 1179656 | tf_op jit(solution)/shard_map/ppermute | solution.py:273
  54.1 11.3 %collective-permute-start.8 = (bf16[64,3072]{1,0:T(8,128)(2,1)S(1)}, bf16[64,3072]{1,0:T(8,128)(2,1)S(1)}, u32[]{:S(2)}, u32[]{:S(2)}) collective-permute-start(bf16[64,3072]{1,0:T(8,128)(2,1)S(1)} %get-tuple-element.20), channel_id=1, source_target_pairs={{0,64},{16,80},{32,96},{48,112},{64,128},{80,144},{96,160},{112,17... | collective-permute-start | bytes 1179656 | tf_op jit(solution)/shard_map/ppermute | solution.py:273
  55.4 10.0 %collective-permute-start.7 = (bf16[64,3072]{1,0:T(8,128)(2,1)S(1)}, bf16[64,3072]{1,0:T(8,128)(2,1)S(1)}, u32[]{:S(2)}, u32[]{:S(2)}) collective-permute-start(bf16[64,3072]{1,0:T(8,128)(2,1)S(1)} %get-tuple-element.20), channel_id=1, source_target_pairs={{0,192},{16,208},{32,224},{48,240},{64,0},{80,16},{96,32},{112,48}... | collective-permute-start | bytes 1179656 | tf_op jit(solution)/shard_map/ppermute | solution.py:273
  57.0 12.6 %copy-start.1 = (bf16[256,3072]{1,0:T(8,128)(2,1)}, bf16[256,3072]{1,0:T(8,128)(2,1)S(1)}, u32[]{:S(2)}) copy-start(bf16[256,3072]{1,0:T(8,128)(2,1)S(1)} %pad_maximum_fusion.1.own_ref) | copy-start | bytes 4718596
  60.9 8.7 %collective-permute-start.10 = (bf16[256,3072]{1,0:T(8,128)(2,1)S(1)}, bf16[256,3072]{1,0:T(8,128)(2,1)}, u32[]{:S(2)}, u32[]{:S(2)}) collective-permute-start(bf16[256,3072]{1,0:T(8,128)(2,1)S(1)} %pad_maximum_fusion.1.own_ref), channel_id=1, source_target_pairs={{0,16},{16,0},{32,48},{48,32},{64,80},{80,64},{96,112},{112,96},{1... | collective-permute-start | bytes 4718600 | tf_op jit(solution)/shard_map/ppermute | solution.py:278
  66.7 10.4 %collective-permute-start.9 = (bf16[256,3072]{1,0:T(8,128)(2,1)}, bf16[256,3072]{1,0:T(8,128)(2,1)}, u32[]{:S(2)}, u32[]{:S(2)}) collective-permute-start(bf16[256,3072]{1,0:T(8,128)(2,1)} %pad_maximum_fusion.own_ref), channel_id=1, source_target_pairs={{0,16},{16,0},{32,48},{48,32},{64,80},{80,64},{96,112},{112,96},{1... | collective-permute-start | bytes 4718600 | tf_op jit(solution)/shard_map/ppermute | solution.py:278
  77.2 7.6 %copy-start.6 = (s32[64,1]{0,1:T(1,128)S(1)}, s32[64,1]{0,1:T(1,128)}, u32[]{:S(2)}) copy-start(s32[64,1]{0,1:T(1,128)} %param.16) | copy-start | bytes 772
  84.9 3.4 %copy-start.7 = (s32[64]{0:T(128)S(1)}, s32[64]{0:T(128)}, u32[]{:S(2)}) copy-start(s32[64]{0:T(128)} %param.15) | copy-start | bytes 772
  91.3 1.6 copy-start.2
  96.3 16.8 %copy-start.8 = (s32[1,128]{1,0:T(1,128)S(1)}, s32[1,128]{1,0:T(1,128)}, u32[]{:S(2)}) copy-start(s32[1,128]{1,0:T(1,128)} %param.17) | copy-start | bytes 1540
  96.8 1.6 collective-permute-start.11
  100.0 8.0 %collective-permute-start.12 = (bf16[4,2,16384]{2,1,0:T(2,128)(2,1)S(1)}, bf16[4,2,16384]{2,1,0:T(2,128)(2,1)S(1)}, u32[]{:S(2)}, u32[]{:S(2)}) collective-permute-start(bf16[4,2,16384]{2,1,0:T(2,128)(2,1)S(1)} %get-tuple-element.31), channel_id=1, source_target_pairs={{0,32},{16,48},{32,0},{48,16},{64,96},{80,112},{96,64},{112,80},{1... | collective-permute-start | bytes 786440 | tf_op jit(solution)/shard_map/ppermute | solution.py:214
  108.7 5.8 %collective-permute-start.13 = (bf16[2,2,16384]{2,1,0:T(2,128)(2,1)S(1)}, bf16[2,2,16384]{2,1,0:T(2,128)(2,1)S(1)}, u32[]{:S(2)}, u32[]{:S(2)}) collective-permute-start(bf16[2,2,16384]{2,1,0:T(2,128)(2,1)S(1)} %get-tuple-element.35), channel_id=1, source_target_pairs={{0,64},{16,80},{32,96},{48,112},{64,128},{80,144},{96,160},{112,17... | collective-permute-start | bytes 393224 | tf_op jit(solution)/shard_map/ppermute | solution.py:215
  110.3 4.2 %collective-permute-start.15 = (bf16[2,2,16384]{2,1,0:T(2,128)(2,1)S(1)}, bf16[2,2,16384]{2,1,0:T(2,128)(2,1)S(1)}, u32[]{:S(2)}, u32[]{:S(2)}) collective-permute-start(bf16[2,2,16384]{2,1,0:T(2,128)(2,1)S(1)} %get-tuple-element.36), channel_id=1, source_target_pairs={{0,192},{16,208},{32,224},{48,240},{64,0},{80,16},{96,32},{112,48}... | collective-permute-start | bytes 393224 | tf_op jit(solution)/shard_map/ppermute | solution.py:215
  111.8 7.0 %collective-permute-start.14 = (bf16[2,2,16384]{2,1,0:T(2,128)(2,1)S(1)}, bf16[2,2,16384]{2,1,0:T(2,128)(2,1)S(1)}, u32[]{:S(2)}, u32[]{:S(2)}) collective-permute-start(bf16[2,2,16384]{2,1,0:T(2,128)(2,1)S(1)} %get-tuple-element.37), channel_id=1, source_target_pairs={{0,128},{16,144},{32,160},{48,176},{64,192},{80,208},{96,224},{112... | collective-permute-start | bytes 393224 | tf_op jit(solution)/shard_map/ppermute | solution.py:215
  124.8 6.9 %copy-start.3 = (bf16[64,1,16,64]{0,3,2,1:T(8,128)(2,1)S(1)}, bf16[64,1,16,64]{0,3,2,1:T(8,128)(2,1)}, u32[]{:S(2)}) copy-start(bf16[64,1,16,64]{0,3,2,1:T(8,128)(2,1)} %copy-done.2) | copy-start | bytes 393220
  129.3 9.0 %copy-start.5 = (bf16[64,4096]{1,0:T(8,128)(2,1)S(1)}, bf16[64,4096]{1,0:T(8,128)(2,1)}, u32[]{:S(2)}) copy-start(bf16[64,4096]{1,0:T(8,128)(2,1)} %reduce-scatter.3.cloned.1.call-done) | copy-start | bytes 1572868
  130.4 8.0 %collective-permute-start.1 = (bf16[64,2048]{1,0:T(8,128)(2,1)S(1)}, bf16[64,2048]{1,0:T(8,128)(2,1)S(1)}, u32[]{:S(2)}, u32[]{:S(2)}) collective-permute-start(bf16[64,2048]{1,0:T(8,128)(2,1)S(1)} %slice.73), channel_id=1, source_target_pairs={{0,8},{1,9},{2,10},{3,11},{4,12},{5,13},{6,14},{7,15},{8,0},{9,1},... | collective-permute-start | bytes 786440 | tf_op jit(solution)/shard_map/ppermute | solution.py:282
Sparse Core Ops, SparseCore 0:
  28.9 57.6 reduce-scatter.2
  89.2 73.7 reduce-scatter.4
